TPU v7x, 32 devices: a whole 2x2x4 slice. The times are simulated.
32 devices in a mesh: seq: 16 (over z, y, x), head: 2 (over core).
Axes of the slice: x: 2, y: 2, z: 4, core: 2. Of those that a mesh axis runs over, the one named last changes fastest.
Arguments:
- query_rows: bfloat16 [32, 4096, 128], P('head', 'seq'), may hold values from -6 to 6
- key_rows: bfloat16 [32, 4096, 128], P('head', 'seq'), may hold values from -0.5 to 0.5
- value_rows: bfloat16 [32, 4096, 128], P('head', 'seq'), may hold values from -40 to 40
- log_gate: float32 [32, 4096], P('head', 'seq'), may hold values from -1 to 0
- episode: int32 [4096], P('seq'), may hold values from 0 to 3, never falling along the last dimension, each value on 1 to 2048 neighbouring positions
- grad_out: bfloat16 [32, 4096, 128], P('head', 'seq'), may hold values from -6 to 6
Outputs:
- normed: bfloat16 [32, 4096, 128], P('head', 'seq')
- grad_query: bfloat16 [32, 4096, 128], P('head', 'seq')
- grad_key: bfloat16 [32, 4096, 128], P('head', 'seq')
- grad_value: bfloat16 [32, 4096, 128], P('head', 'seq')
Inputs may be any that keep to these rules, and one draw needn't show every extreme that they name: Episode ids never fall along the tokens; every episode spans 1 to 2048 tokens and one spans exactly 2048.
All inputs are finite; a program needn't handle non-finite values.
Results may differ from a plain program's by a relative error of at most 0.0062.
Values sent between devices are 32-bit elements; how exact they have to be, the bound alone decides.
A program may use at most 64 MiB of HBM per device.

v0:
```python
import jax
import jax.numpy as jnp
from jax import lax
from jax.sharding import PartitionSpec as P

STRETCH = 256
REACH_MAX = 16


EPSILON = 1e-06


def passed_along(block, axis, distance):
    devices = range(lax.axis_size(axis))
    route = [(i - distance, i) for i in devices if i - distance in devices]
    return lax.ppermute(block, axis, route)


def forward_join(earlier, latter):
    early_total, early_state, early_mark = earlier
    late_total, late_state, late_mark = latter
    empty_late = late_mark < 0
    carried = jnp.where(
        early_mark == late_mark, jnp.exp(late_total)[:, None, None] * early_state, 0.0
    )
    joined_state = jnp.where(empty_late, early_state, late_state + carried)
    joined_mark = jnp.where(empty_late, early_mark, late_mark)
    return (early_total + late_total, joined_state, joined_mark)


def reverse_merge_pass(earlier, latter):
    early_total, early_state, early_mark = earlier
    late_total, late_state, late_mark = latter
    empty_late = late_mark < 0
    carried = jnp.where(
        late_mark == early_mark, jnp.exp(late_total)[:, None, None] * early_state, 0.0
    )
    joined_state = jnp.where(empty_late, early_state, late_state + carried)
    joined_mark = jnp.where(empty_late, early_mark, late_mark)
    return (early_total + late_total, joined_state, joined_mark)


def shift_forward(payload, distance):
    return passed_along(payload, "seq", distance)


def shift_backward(payload, distance):
    return passed_along(payload, "seq", -distance)


def window_prefix(own_part, joiner, shifter):
    window_span = min(REACH_MAX, lax.axis_size("seq") // 2)
    levels = (window_span - 1).bit_length()
    gathered = shifter(own_part, 1)
    for degree in range(levels):
        received = shifter(gathered, 1 << degree)
        gathered = joiner(received, gathered)
    return gathered


def per_device(query_rows, key_rows, value_rows, log_gate, episode, grad_out):
    head_count, tokens, head_width = query_rows.shape
    stretch_count = tokens // STRETCH

    def partition_sets(values):
        return values.reshape(head_count, stretch_count, STRETCH, head_width)

    queries = partition_sets(query_rows)
    keyset = partition_sets(key_rows)
    values = partition_sets(value_rows)
    cotangent = partition_sets(grad_out)
    running = jnp.cumsum(log_gate.reshape(head_count, stretch_count, STRETCH), axis=-1)
    episodes = episode.reshape(stretch_count, STRETCH)
    causal = jnp.arange(STRETCH)[:, None] >= jnp.arange(STRETCH)[None, :]
    allowed = ((episodes[:, :, None] == episodes[:, None, :]) & causal[None])[None]
    differences = running[..., :, None] - running[..., None, :]
    decays = jnp.where(allowed, jnp.exp(jnp.where(allowed, differences, 0.0)), 0.0)
    scores = (
        jnp.einsum("hncd,hnsd->hncs", queries, keyset, preferred_element_type=jnp.float32) * decays
    ).astype(jnp.bfloat16)
    within = jnp.einsum("hncs,hnse->hnce", scores, values, preferred_element_type=jnp.float32)
    totals = running[..., -1]
    last_ids = episodes[:, -1]
    weight = jnp.where(
        (episodes == last_ids[:, None])[None], jnp.exp(running[..., -1:] - running), 0.0
    )
    keys_decayed = (keyset * weight[..., None]).astype(jnp.bfloat16)
    local_states = jnp.einsum(
        "hncd,hnce->hnde", keys_decayed, values, preferred_element_type=jnp.float32
    )
    stretch_parts = (totals[:, 0], local_states[:, 0], last_ids[0])
    incoming = window_prefix(stretch_parts, forward_join, shift_forward)
    entering = [incoming]
    state_low = jnp.stack([member[1] for member in entering], axis=1).astype(jnp.bfloat16)
    prior_ids = jnp.stack([member[2] for member in entering])
    carried = jnp.where((episodes == prior_ids[:, None])[None], jnp.exp(running), 0.0)
    attention = (
        within
        + jnp.einsum("hncd,hnde->hnce", queries, state_low, preferred_element_type=jnp.float32)
        * carried[..., None]
    )
    cotangent_wide = cotangent.astype(jnp.float32)
    squared_terms = jnp.sum(attention * attention, axis=(0, 3))
    crossed = jnp.sum(cotangent_wide * attention, axis=(0, 3))
    squared_terms, crossed = lax.psum((squared_terms, crossed), "head")
    features = head_count * lax.axis_size("head") * head_width
    root_mean = jnp.sqrt(squared_terms / features + EPSILON)
    normed = (attention / root_mean[None, :, :, None]).astype(jnp.bfloat16)
    grad_attn = (
        (
            cotangent_wide
            - attention * (crossed / (features * root_mean * root_mean))[None, :, :, None]
        )
        / root_mean[None, :, :, None]
    ).astype(jnp.bfloat16)
    score_gradient = (
        jnp.einsum("hnce,hnse->hncs", grad_attn, values, preferred_element_type=jnp.float32)
        * decays
    ).astype(jnp.bfloat16)
    first_ids = episodes[:, 0]
    query_weight = jnp.where((episodes == first_ids[:, None])[None], jnp.exp(running), 0.0)
    queries_decayed = (queries * query_weight[..., None]).astype(jnp.bfloat16)
    back_local = jnp.einsum(
        "hncd,hnce->hnde", queries_decayed, grad_attn, preferred_element_type=jnp.float32
    )
    back_parts = [(totals[:, 0], back_local[:, 0], first_ids[0])]
    back_summary = back_parts[stretch_count - 1]
    arriving = window_prefix(back_summary, reverse_merge_pass, shift_backward)
    query_grad = (
        jnp.einsum("hncs,hnsd->hncd", score_gradient, keyset, preferred_element_type=jnp.float32)
        + jnp.einsum("hnce,hnde->hncd", grad_attn, state_low, preferred_element_type=jnp.float32)
        * carried[..., None]
    )
    key_inner = jnp.einsum(
        "hncs,hncd->hnsd", score_gradient, queries, preferred_element_type=jnp.float32
    )
    value_inner = jnp.einsum(
        "hncs,hnce->hnse", scores, grad_attn, preferred_element_type=jnp.float32
    )
    leaving = [arriving]
    back_low = jnp.stack([member[1] for member in leaving], axis=1).astype(jnp.bfloat16)
    next_ids = jnp.stack([member[2] for member in leaving])
    trailing = jnp.where(
        (episodes == next_ids[:, None])[None], jnp.exp(running[..., -1:] - running), 0.0
    )
    key_grad = (
        key_inner
        + jnp.einsum("hnce,hnde->hncd", values, back_low, preferred_element_type=jnp.float32)
        * trailing[..., None]
    )
    value_grad = (
        value_inner
        + jnp.einsum("hncd,hnde->hnce", keyset, back_low, preferred_element_type=jnp.float32)
        * trailing[..., None]
    )

    def unblock(values_in):
        return values_in.reshape(head_count, tokens, head_width).astype(jnp.bfloat16)

    return (unblock(normed), unblock(query_grad), unblock(key_grad), unblock(value_grad))


def solution(mesh):
    placed = (
        P("head", "seq", None),
        P("head", "seq", None),
        P("head", "seq", None),
        P("head", "seq"),
        P("seq"),
        P("head", "seq", None),
    )
    return jax.shard_map(
        per_device,
        mesh=mesh,
        in_specs=placed,
        out_specs=(
            P("head", "seq", None),
            P("head", "seq", None),
            P("head", "seq", None),
            P("head", "seq", None),
        ),
        check_vma=False,
    )
```

profile of v0, /device:TPU:0, one launch (start us, length us, event | category | flops | bytes accessed | tf_op | source)
XLA Modules:
  0.0 285.0 jit_solution(5547450861218648079)
XLA Ops:
  0.6 1.3 fusion.16
  2.0 5.4 %collective-permute-start = (s32[]{:T(128)}, s32[]{:T(128)}, u32[]{:S(2)}, u32[]{:S(2)}) collective-permute-start(s32[]{:T(128)} %bitcast.2), channel_id=1, source_target_pairs={{0,2},{2,4},{4,6},{6,8},{8,10},{10,12},{12,14},{14,16},{16,18},{18... | collective-permute-start | bytes 20 | tf_op jit(solution)/shard_map/ppermute | solution.py:16
  7.4 1.3 collective-permute-start.11
  8.7 0.7 reshape.426
  9.4 0.6 reduce-window.6
  10.0 0.2 slice_reduce_fusion
  10.4 0.3 fusion.12
  10.7 5.1 %collective-permute-start.1 = (s32[]{:T(128)}, s32[]{:T(128)}, u32[]{:S(2)}, u32[]{:S(2)}) collective-permute-start(s32[]{:T(128)} %collective-permute-done), channel_id=1, source_target_pairs={{0,2},{2,4},{4,6},{6,8},{8,10},{10,12},{12,14},{14,16},{16,18},{18... | collective-permute-start | bytes 20 | tf_op jit(solution)/shard_map/ppermute | solution.py:16
  17.1 1.3 collective-permute-start.12
  19.7 6.6 %collective-permute-start.2 = (s32[]{:T(128)}, s32[]{:T(128)}, u32[]{:S(2)}, u32[]{:S(2)}) collective-permute-start(s32[]{:T(128)} %select_n.143), channel_id=1, source_target_pairs={{0,4},{2,6},{4,8},{6,10},{8,12},{10,14},{12,16},{14,18},{16,20},{1... | collective-permute-start | bytes 20 | tf_op jit(solution)/shard_map/ppermute | solution.py:16
  27.7 1.3 collective-permute-start.13
  29.7 9.9 %collective-permute-start.9 = (s32[]{:T(128)}, s32[]{:T(128)}, u32[]{:S(2)}, u32[]{:S(2)}) collective-permute-start(s32[]{:T(128)} %select_n.144), channel_id=1, source_target_pairs={{0,8},{2,10},{4,12},{6,14},{8,16},{10,18},{12,20},{14,22},{16,24},... | collective-permute-start | bytes 20 | tf_op jit(solution)/shard_map/ppermute | solution.py:16
  40.1 1.3 collective-permute-start.20
  42.0 3.6 %collective-permute-done.20 = s32[]{:T(128)} collective-permute-done((s32[]{:T(128)}, s32[]{:T(128)}, u32[]{:S(2)}, u32[]{:S(2)}) %collective-permute-start.20) | collective-permute-done | bytes 36 | tf_op jit(solution)/shard_map/ppermute | solution.py:16
  46.3 2.0 broadcast_compare_fusion.1
  48.4 2.6 fusion.5
  51.0 1.4 collective-permute-start.3
  52.4 18.9 %collective-permute-done.3 = f32[16,128,128]{2,1,0:T(8,128)S(1)} collective-permute-done((f32[16,128,128]{2,1,0:T(8,128)S(1)}, f32[16,128,128]{2,1,0:T(8,128)S(1)}, u32[]{:S(2)}, u32[]{:S(2)}) %collective-permute-start.3) | collective-permute-done | bytes 1048608 | tf_op jit(solution)/shard_map/ppermute | solution.py:16
  71.3 4.4 %collective-permute-start.4 = (f32[16,128,128]{2,1,0:T(8,128)S(1)}, f32[16,128,128]{2,1,0:T(8,128)S(1)}, u32[]{:S(2)}, u32[]{:S(2)}) collective-permute-start(f32[16,128,128]{2,1,0:T(8,128)S(1)} %collective-permute-done.3), channel_id=1, source_target_pairs={{0,2},{2,4},{4,6},{6,8},{8,10},{10,12},{12,14},{14,16},{16,18},{18... | collective-permute-start | bytes 3145736 | tf_op jit(solution)/shard_map/ppermute | solution.py:16
  75.7 4.0 %collective-permute-start.5 = (f32[16]{0:T(128)S(1)}, f32[16]{0:T(128)S(1)}, u32[]{:S(2)}, u32[]{:S(2)}) collective-permute-start(f32[16]{0:T(128)S(1)} %fusion.12), channel_id=1, source_target_pairs={{0,2},{2,4},{4,6},{6,8},{8,10},{10,12},{12,14},{14,16},{16,18},{18... | collective-permute-start | bytes 200 | tf_op jit(solution)/shard_map/ppermute | solution.py:16
  79.8 12.8 %collective-permute-done.5 = f32[16]{0:T(128)S(1)} collective-permute-done((f32[16]{0:T(128)S(1)}, f32[16]{0:T(128)S(1)}, u32[]{:S(2)}, u32[]{:S(2)}) %collective-permute-start.5) | collective-permute-done | bytes 96 | tf_op jit(solution)/shard_map/ppermute | solution.py:16
  92.5 4.4 %collective-permute-start.7 = (f32[16]{0:T(128)S(1)}, f32[16]{0:T(128)S(1)}, u32[]{:S(2)}, u32[]{:S(2)}) collective-permute-start(f32[16]{0:T(128)S(1)} %collective-permute-done.5), channel_id=1, source_target_pairs={{0,2},{2,4},{4,6},{6,8},{8,10},{10,12},{12,14},{14,16},{16,18},{18... | collective-permute-start | bytes 200 | tf_op jit(solution)/shard_map/ppermute | solution.py:16
  98.2 1.0 copy-done.9
  99.2 1.4 add_select_fusion.3
  100.6 6.8 %collective-permute-start.6 = (f32[16,128,128]{2,1,0:T(8,128)S(1)}, f32[16,128,128]{2,1,0:T(8,128)S(1)}, u32[]{:S(2)}, u32[]{:S(2)}) collective-permute-start(f32[16,128,128]{2,1,0:T(8,128)S(1)} %add_select_fusion.3), channel_id=1, source_target_pairs={{0,4},{2,6},{4,8},{6,10},{8,12},{10,14},{12,16},{14,18},{16,20},{1... | collective-permute-start | bytes 3145736 | tf_op jit(solution)/shard_map/ppermute | solution.py:16
  108.1 14.3 %collective-permute-done.6 = f32[16,128,128]{2,1,0:T(8,128)S(1)} collective-permute-done((f32[16,128,128]{2,1,0:T(8,128)S(1)}, f32[16,128,128]{2,1,0:T(8,128)S(1)}, u32[]{:S(2)}, u32[]{:S(2)}) %collective-permute-start.6) | collective-permute-done | bytes 1048608 | tf_op jit(solution)/shard_map/ppermute | solution.py:16
  122.4 1.0 copy-done.10
  123.4 2.5 add_select_fusion.2
  125.9 10.6 %collective-permute-start.8 = (f32[16,128,128]{2,1,0:T(8,128)}, f32[16,128,128]{2,1,0:T(8,128)}, u32[]{:S(2)}, u32[]{:S(2)}) collective-permute-start(f32[16,128,128]{2,1,0:T(8,128)} %add_select_fusion.2), channel_id=1, source_target_pairs={{0,8},{2,10},{4,12},{6,14},{8,16},{10,18},{12,20},{14,22},{16,24},... | collective-permute-start | bytes 3145736 | tf_op jit(solution)/shard_map/ppermute | solution.py:16
  136.5 0.1 fusion.9
  136.6 1.5 copy.53
  138.1 2.9 %multiply_convert_fusion.1 = bf16[16,256,256]{2,1,0:T(8,128)(2,1)S(1)} fusion(bf16[16,256,128]{2,1,0:T(8,128)(2,1)S(1)} %copy-done.1, bf16[16,256,128]{2,1,0:T(8,128)(2,1)} %param.7, f32[16,256]{1,0:T(8,128)S(1)} %get-tuple-element.21, pred[256,256]{1,0:T(8,128)(4,1)S(1)} %fusion.9), kind=kOutput, calls=%fused_computation.1 | convolution fusion | flops 273678336 | bytes 4276224 | tf_op jit(solution)/shard_map/hncd,hnsd->hncs/dot_general | solution.py:79
  141.0 2.1 fusion.17
  143.2 1.3 collective-permute-start.10
  145.1 0.7 collective-permute-done.10
  145.7 2.4 collective-permute-done.8
  148.1 1.8 select_convert_fusion.1
  149.9 2.1 fusion
  152.0 2.4 all-reduce
  154.5 3.4 %fusion.2 = (bf16[16,256,128]{1,2,0:T(8,128)(2,1)S(1)}, bf16[16,256,128]{1,2,0:T(8,128)(2,1)}) fusion(bf16[16,256,128]{1,2,0:T(8,128)(2,1)} %copy-done.2, f32[16,256,128]{1,2,0:T(8,128)} %get-tuple-element.41, f32[256]{0:T(256)S(1)} %bitcast.61, f32[256]{0:T(256)S(1)} %bitcast.62), kind=kLoop, calls=%fused_computation.7 | loop fusion | flops 3670016 | bytes 5244928 | tf_op jit(solution)/shard_map/convert_element_type | solution.py:115
  157.9 1.6 fusion.6
  159.5 1.3 collective-permute-start.14
  160.8 25.9 %collective-permute-done.14 = f32[16,128,128]{2,1,0:T(8,128)} collective-permute-done((f32[16,128,128]{2,1,0:T(8,128)S(1)}, f32[16,128,128]{2,1,0:T(8,128)}, u32[]{:S(2)}, u32[]{:S(2)}) %collective-permute-start.14) | collective-permute-done | bytes 1048608 | tf_op jit(solution)/shard_map/ppermute | solution.py:16
  186.8 1.3 collective-permute-start.15
  188.0 1.3 collective-permute-start.16
  189.3 24.0 %collective-permute-done.16 = f32[16]{0:T(128)S(1)} collective-permute-done((f32[16]{0:T(128)S(1)}, f32[16]{0:T(128)S(1)}, u32[]{:S(2)}, u32[]{:S(2)}) %collective-permute-start.16) | collective-permute-done | bytes 96 | tf_op jit(solution)/shard_map/ppermute | solution.py:16
  213.4 1.3 collective-permute-start.18
  216.0 2.9 %collective-permute-done.18 = f32[16]{0:T(128)S(1)} collective-permute-done((f32[16]{0:T(128)S(1)}, f32[16]{0:T(128)S(1)}, u32[]{:S(2)}, u32[]{:S(2)}) %collective-permute-start.18) | collective-permute-done | bytes 96 | tf_op jit(solution)/shard_map/ppermute | solution.py:16
  218.9 2.7 add_select_fusion.1
  221.6 1.3 collective-permute-start.17
  223.5 1.3 collective-permute-start.21
  225.4 23.8 %collective-permute-done.21 = f32[16]{0:T(128)S(1)} collective-permute-done((f32[16]{0:T(128)S(1)}, f32[16]{0:T(128)S(1)}, u32[]{:S(2)}, u32[]{:S(2)}) %collective-permute-start.21) | collective-permute-done | bytes 96 | tf_op jit(solution)/shard_map/ppermute | solution.py:16
  249.2 2.3 copy.64
  251.5 1.5 multiply_convert_fusion
  253.0 0.7 fusion.18
  253.7 1.8 add_select_fusion
  255.6 1.6 collective-permute-start.19
  257.2 1.9 add_convert_fusion
  259.1 0.8 fusion.20
  259.8 0.8 fusion.19
  260.6 21.0 %collective-permute-done.19 = f32[16,128,128]{2,1,0:T(8,128)S(1)} collective-permute-done((f32[16,128,128]{2,1,0:T(8,128)S(1)}, f32[16,128,128]{2,1,0:T(8,128)S(1)}, u32[]{:S(2)}, u32[]{:S(2)}) %collective-permute-start.19) | collective-permute-done | bytes 1048608 | tf_op jit(solution)/shard_map/ppermute | solution.py:16
  281.6 0.2 select_convert_fusion
  281.8 1.6 fusion.3
  283.4 1.5 fusion.4
  (47 shorter events, 0.5 us)
Async XLA Ops:
  0.6 47.8 %copy-start = (bf16[16,256,128]{2,1,0:T(8,128)(2,1)S(1)}, bf16[16,256,128]{2,1,0:T(8,128)(2,1)}, u32[]{:S(2)}) copy-start(bf16[16,256,128]{2,1,0:T(8,128)(2,1)} %param.8) | copy-start | bytes 3145732
  2.0 8.7 %collective-permute-start = (s32[]{:T(128)}, s32[]{:T(128)}, u32[]{:S(2)}, u32[]{:S(2)}) collective-permute-start(s32[]{:T(128)} %bitcast.2), channel_id=1, source_target_pairs={{0,2},{2,4},{4,6},{6,8},{8,10},{10,12},{12,14},{14,16},{16,18},{18... | collective-permute-start | bytes 20 | tf_op jit(solution)/shard_map/ppermute | solution.py:16
  7.4 9.0 %collective-permute-start.11 = (s32[]{:T(128)}, s32[]{:T(128)}, u32[]{:S(2)}, u32[]{:S(2)}) collective-permute-start(s32[]{:T(128)} %bitcast.10), channel_id=1, source_target_pairs={{2,0},{4,2},{6,4},{8,6},{10,8},{12,10},{14,12},{16,14},{18,16},{20... | collective-permute-start | bytes 20 | tf_op jit(solution)/shard_map/ppermute | solution.py:16
  10.7 7.7 %collective-permute-start.1 = (s32[]{:T(128)}, s32[]{:T(128)}, u32[]{:S(2)}, u32[]{:S(2)}) collective-permute-start(s32[]{:T(128)} %collective-permute-done), channel_id=1, source_target_pairs={{0,2},{2,4},{4,6},{6,8},{8,10},{10,12},{12,14},{14,16},{16,18},{18... | collective-permute-start | bytes 20 | tf_op jit(solution)/shard_map/ppermute | solution.py:16
  17.1 9.2 %collective-permute-start.12 = (s32[]{:T(128)}, s32[]{:T(128)}, u32[]{:S(2)}, u32[]{:S(2)}) collective-permute-start(s32[]{:T(128)} %collective-permute-done.11), channel_id=1, source_target_pairs={{2,0},{4,2},{6,4},{8,6},{10,8},{12,10},{14,12},{16,14},{18,16},{20... | collective-permute-start | bytes 20 | tf_op jit(solution)/shard_map/ppermute | solution.py:16
  19.7 9.3 %collective-permute-start.2 = (s32[]{:T(128)}, s32[]{:T(128)}, u32[]{:S(2)}, u32[]{:S(2)}) collective-permute-start(s32[]{:T(128)} %select_n.143), channel_id=1, source_target_pairs={{0,4},{2,6},{4,8},{6,10},{8,12},{10,14},{12,16},{14,18},{16,20},{1... | collective-permute-start | bytes 20 | tf_op jit(solution)/shard_map/ppermute | solution.py:16
  27.7 11.9 %collective-permute-start.13 = (s32[]{:T(128)}, s32[]{:T(128)}, u32[]{:S(2)}, u32[]{:S(2)}) collective-permute-start(s32[]{:T(128)} %select_n.160), channel_id=1, source_target_pairs={{4,0},{6,2},{8,4},{10,6},{12,8},{14,10},{16,12},{18,14},{20,16},{2... | collective-permute-start | bytes 20 | tf_op jit(solution)/shard_map/ppermute | solution.py:16
  29.7 11.7 %collective-permute-start.9 = (s32[]{:T(128)}, s32[]{:T(128)}, u32[]{:S(2)}, u32[]{:S(2)}) collective-permute-start(s32[]{:T(128)} %select_n.144), channel_id=1, source_target_pairs={{0,8},{2,10},{4,12},{6,14},{8,16},{10,18},{12,20},{14,22},{16,24},... | collective-permute-start | bytes 20 | tf_op jit(solution)/shard_map/ppermute | solution.py:16
  40.1 5.5 %collective-permute-start.20 = (s32[]{:T(128)}, s32[]{:T(128)}, u32[]{:S(2)}, u32[]{:S(2)}) collective-permute-start(s32[]{:T(128)} %select_n.161), channel_id=1, source_target_pairs={{8,0},{10,2},{12,4},{14,6},{16,8},{18,10},{20,12},{22,14},{24,16},... | collective-permute-start | bytes 20 | tf_op jit(solution)/shard_map/ppermute | solution.py:16
  51.0 20.2 %collective-permute-start.3 = (f32[16,128,128]{2,1,0:T(8,128)S(1)}, f32[16,128,128]{2,1,0:T(8,128)S(1)}, u32[]{:S(2)}, u32[]{:S(2)}) collective-permute-start(f32[16,128,128]{2,1,0:T(8,128)S(1)} %fusion.5), channel_id=1, source_target_pairs={{0,2},{2,4},{4,6},{6,8},{8,10},{10,12},{12,14},{14,16},{16,18},{18... | collective-permute-start | bytes 3145736 | tf_op jit(solution)/shard_map/ppermute | solution.py:16
  71.3 27.0 %collective-permute-start.4 = (f32[16,128,128]{2,1,0:T(8,128)S(1)}, f32[16,128,128]{2,1,0:T(8,128)S(1)}, u32[]{:S(2)}, u32[]{:S(2)}) collective-permute-start(f32[16,128,128]{2,1,0:T(8,128)S(1)} %collective-permute-done.3), channel_id=1, source_target_pairs={{0,2},{2,4},{4,6},{6,8},{8,10},{10,12},{12,14},{14,16},{16,18},{18... | collective-permute-start | bytes 3145736 | tf_op jit(solution)/shard_map/ppermute | solution.py:16
  75.7 16.8 %collective-permute-start.5 = (f32[16]{0:T(128)S(1)}, f32[16]{0:T(128)S(1)}, u32[]{:S(2)}, u32[]{:S(2)}) collective-permute-start(f32[16]{0:T(128)S(1)} %fusion.12), channel_id=1, source_target_pairs={{0,2},{2,4},{4,6},{6,8},{8,10},{10,12},{12,14},{14,16},{16,18},{18... | collective-permute-start | bytes 200 | tf_op jit(solution)/shard_map/ppermute | solution.py:16
  92.5 5.7 %collective-permute-start.7 = (f32[16]{0:T(128)S(1)}, f32[16]{0:T(128)S(1)}, u32[]{:S(2)}, u32[]{:S(2)}) collective-permute-start(f32[16]{0:T(128)S(1)} %collective-permute-done.5), channel_id=1, source_target_pairs={{0,2},{2,4},{4,6},{6,8},{8,10},{10,12},{12,14},{14,16},{16,18},{18... | collective-permute-start | bytes 200 | tf_op jit(solution)/shard_map/ppermute | solution.py:16
  98.2 1.0 copy-start.9
  100.6 35.8 %copy-start.11 = (s32[256]{0:T(256)S(1)}, s32[256]{0:T(256)}, u32[]{:S(2)}) copy-start(s32[256]{0:T(256)} %param.10) | copy-start | bytes 3076
  100.6 21.8 %collective-permute-start.6 = (f32[16,128,128]{2,1,0:T(8,128)S(1)}, f32[16,128,128]{2,1,0:T(8,128)S(1)}, u32[]{:S(2)}, u32[]{:S(2)}) collective-permute-start(f32[16,128,128]{2,1,0:T(8,128)S(1)} %add_select_fusion.3), channel_id=1, source_target_pairs={{0,4},{2,6},{4,8},{6,10},{8,12},{10,14},{12,16},{14,18},{16,20},{1... | collective-permute-start | bytes 3145736 | tf_op jit(solution)/shard_map/ppermute | solution.py:16
  122.4 1.0 copy-start.10
  123.4 14.7 %copy-start.1 = (bf16[16,256,128]{2,1,0:T(8,128)(2,1)S(1)}, bf16[16,256,128]{2,1,0:T(8,128)(2,1)}, u32[]{:S(2)}) copy-start(bf16[16,256,128]{2,1,0:T(8,128)(2,1)} %param.6) | copy-start | bytes 3145732
  125.9 22.2 %collective-permute-start.8 = (f32[16,128,128]{2,1,0:T(8,128)}, f32[16,128,128]{2,1,0:T(8,128)}, u32[]{:S(2)}, u32[]{:S(2)}) collective-permute-start(f32[16,128,128]{2,1,0:T(8,128)} %add_select_fusion.2), channel_id=1, source_target_pairs={{0,8},{2,10},{4,12},{6,14},{8,16},{10,18},{12,20},{14,22},{16,24},... | collective-permute-start | bytes 3145736 | tf_op jit(solution)/shard_map/ppermute | solution.py:16
  138.1 11.8 %copy-start.2 = (bf16[16,256,128]{1,2,0:T(8,128)(2,1)}, bf16[16,256,128]{1,2,0:T(8,128)(2,1)S(1)}, u32[]{:S(2)}) copy-start(bf16[16,256,128]{1,2,0:T(8,128)(2,1)S(1)} %copy.53) | copy-start | bytes 3145732
  141.0 2.2 copy-start.4
  143.2 2.6 collective-permute-start.10
  145.1 4.8 %copy-start.6 = (f32[16,256,128]{1,2,0:T(8,128)S(1)}, f32[16,256,128]{1,2,0:T(8,128)}, u32[]{:S(2)}) copy-start(f32[16,256,128]{1,2,0:T(8,128)} %fusion.17) | copy-start | bytes 6291460
  149.9 2.1 copy-start.7
  159.5 27.2 %collective-permute-start.14 = (f32[16,128,128]{2,1,0:T(8,128)S(1)}, f32[16,128,128]{2,1,0:T(8,128)}, u32[]{:S(2)}, u32[]{:S(2)}) collective-permute-start(f32[16,128,128]{2,1,0:T(8,128)S(1)} %fusion.6), channel_id=1, source_target_pairs={{2,0},{4,2},{6,4},{8,6},{10,8},{12,10},{14,12},{16,14},{18,16},{20... | collective-permute-start | bytes 3145736 | tf_op jit(solution)/shard_map/ppermute | solution.py:16
  186.8 32.2 %collective-permute-start.15 = (f32[16,128,128]{2,1,0:T(8,128)}, f32[16,128,128]{2,1,0:T(8,128)}, u32[]{:S(2)}, u32[]{:S(2)}) collective-permute-start(f32[16,128,128]{2,1,0:T(8,128)} %collective-permute-done.14), channel_id=1, source_target_pairs={{2,0},{4,2},{6,4},{8,6},{10,8},{12,10},{14,12},{16,14},{18,16},{20... | collective-permute-start | bytes 3145736 | tf_op jit(solution)/shard_map/ppermute | solution.py:16
  188.0 25.3 %collective-permute-start.16 = (f32[16]{0:T(128)S(1)}, f32[16]{0:T(128)S(1)}, u32[]{:S(2)}, u32[]{:S(2)}) collective-permute-start(f32[16]{0:T(128)S(1)} %fusion.12), channel_id=1, source_target_pairs={{2,0},{4,2},{6,4},{8,6},{10,8},{12,10},{14,12},{16,14},{18,16},{20... | collective-permute-start | bytes 200 | tf_op jit(solution)/shard_map/ppermute | solution.py:16
  213.4 5.5 %collective-permute-start.18 = (f32[16]{0:T(128)S(1)}, f32[16]{0:T(128)S(1)}, u32[]{:S(2)}, u32[]{:S(2)}) collective-permute-start(f32[16]{0:T(128)S(1)} %collective-permute-done.16), channel_id=1, source_target_pairs={{2,0},{4,2},{6,4},{8,6},{10,8},{12,10},{14,12},{16,14},{18,16},{20... | collective-permute-start | bytes 200 | tf_op jit(solution)/shard_map/ppermute | solution.py:16
  221.6 32.1 %collective-permute-start.17 = (f32[16,128,128]{2,1,0:T(8,128)}, f32[16,128,128]{2,1,0:T(8,128)}, u32[]{:S(2)}, u32[]{:S(2)}) collective-permute-start(f32[16,128,128]{2,1,0:T(8,128)} %add_select_fusion.1), channel_id=1, source_target_pairs={{4,0},{6,2},{8,4},{10,6},{12,8},{14,10},{16,12},{18,14},{20,16},{2... | collective-permute-start | bytes 3145736 | tf_op jit(solution)/shard_map/ppermute | solution.py:16
  223.5 25.7 %collective-permute-start.21 = (f32[16]{0:T(128)S(1)}, f32[16]{0:T(128)S(1)}, u32[]{:S(2)}, u32[]{:S(2)}) collective-permute-start(f32[16]{0:T(128)S(1)} %get-tuple-element.23), channel_id=1, source_target_pairs={{4,0},{6,2},{8,4},{10,6},{12,8},{14,10},{16,12},{18,14},{20,16},{2... | collective-permute-start | bytes 200 | tf_op jit(solution)/shard_map/ppermute | solution.py:16
  251.5 1.5 copy-start.3
  253.7 3.5 %copy-start.8 = (bf16[16,128,128]{2,1,0:T(8,128)(2,1)S(1)}, bf16[16,128,128]{2,1,0:T(8,128)(2,1)}, u32[]{:S(2)}) copy-start(bf16[16,128,128]{2,1,0:T(8,128)(2,1)} %copy-done.7) | copy-start | bytes 1572868
  255.6 3.5 %copy-start.5 = (bf16[16,256,256]{2,1,0:T(8,128)(2,1)S(1)}, bf16[16,256,256]{2,1,0:T(8,128)(2,1)}, u32[]{:S(2)}) copy-start(bf16[16,256,256]{2,1,0:T(8,128)(2,1)} %copy-done.4) | copy-start | bytes 6291460
  255.6 26.0 %collective-permute-start.19 = (f32[16,128,128]{2,1,0:T(8,128)S(1)}, f32[16,128,128]{2,1,0:T(8,128)S(1)}, u32[]{:S(2)}, u32[]{:S(2)}) collective-permute-start(f32[16,128,128]{2,1,0:T(8,128)S(1)} %add_select_fusion), channel_id=1, source_target_pairs={{8,0},{10,2},{12,4},{14,6},{16,8},{18,10},{20,12},{22,14},{24,16},... | collective-permute-start | bytes 3145736 | tf_op jit(solution)/shard_map/ppermute | solution.py:16
where the time goes:
time: 286 us; the launch traced here: 285 us
  waiting for transfers between devices  150 us (52%)
  starting transfers between devices  74.3 us (26%)
  matrix products  20.1 us (7%)
  other arithmetic  17.1 us (6%)
  between operations  12.6 us (4%)
  local copies, waits for them, and re-layouts  8.17 us (3%)
    ppermute x22, waiting for transfers between devices, passed_along(): return lax.ppermute(block, axis, route)  150 us
    ppermute x22, starting transfers between devices, passed_along(): return lax.ppermute(block, axis, route)  74.3 us
    unnamed x26, local copies, waits for them, and re-layouts  5.74 us
  transfers between devices with their start and end apart: 22, of which 11 were waited for; matrix products, arithmetic and copies ran while one was open for 6% of the time, Pallas kernels for 0%

commit v1 on v0

v1 whole, which is shorter than its diff:
```python
import functools

import jax
import jax.numpy as jnp
from jax import lax
from jax.experimental import pallas as pl
from jax.experimental.pallas import tpu as pltpu
from jax.sharding import PartitionSpec as P

EPSILON = 1e-06
GROUP = 4
BLOCKED = -1e30
MIB = 1 << 20
F32 = jnp.float32
BF16 = jnp.bfloat16
MESH = pl.DeviceIdType.MESH


def product(a, b, over_a, over_b):
    return lax.dot_general(a, b, (((over_a,), (over_b,)), ((), ())), preferred_element_type=F32)


def kernel(
    nseq, nhead, features,
    q_ref, k_ref, v_ref, gate_ref, ep_ref, go_ref,
    normed_ref, gq_ref, gk_ref, gv_ref,
    run_ref, runc_ref, grow_ref, fall_ref, keep_ref, allow_ref, epc_ref, decay_ref, score_ref,
    att_ref, gattn_ref, kin_ref, vin_ref, sums_ref, stat_ref, other_ref, norm_ref, corr_ref,
    ids_ref, prev_ref, next_ref,
    local_ref, group_ref, chain_ref, leave_ref, enter_ref, state_ref,
    blocal_ref, bgroup_ref, bchain_ref, bleave_ref, benter_ref, bstate_ref,
    id_send, id_recv, stat_send, stat_recv,
    up_send, up_recv, chain_send, chain_recv, down_send, down_recv,
    bup_send, bup_recv, bchain_send, bchain_recv, bdown_send, bdown_recv,
):
    heads, tokens, width = q_ref.shape
    owned = heads // GROUP
    groups = nseq // GROUP
    s = lax.axis_index("seq")
    hd = lax.axis_index("head")
    c = lax.rem(s, GROUP)
    z = s // GROUP
    base = s - c

    def member(position):
        return {"seq": base + position}

    def other(distance):
        return lax.rem(c + distance, GROUP)

    barrier = pltpu.get_barrier_semaphore()

    def greet(device):
        pl.semaphore_signal(barrier, inc=1, device_id=device, device_id_type=MESH)

    for d in range(1, GROUP):
        greet(member(other(d)))
    for d in range(1, nhead):
        greet({"head": lax.rem(hd + d, nhead)})

    @pl.when(s > 0)
    def _():
        greet({"seq": s - 1})

    @pl.when(s < nseq - 1)
    def _():
        greet({"seq": s + 1})

    @pl.when(z > 0)
    def _():
        greet({"seq": s - GROUP})

    @pl.when(z < groups - 1)
    def _():
        greet({"seq": s + GROUP})

    lane = lax.broadcasted_iota(jnp.int32, gate_ref.shape, 1)
    run = gate_ref[...]
    step = 1
    while step < tokens:
        run = run + jnp.where(lane >= step, pltpu.roll(run, step, 1), 0.0)
        step *= 2
    run_ref[...] = run
    total = run[:, tokens - 1 : tokens]
    columns = run.T
    grown = jnp.exp(run).T
    fallen = jnp.exp(total - run).T
    for h in range(heads):
        runc_ref[h] = jnp.broadcast_to(columns[:, h : h + 1], (tokens, width))
        grow_ref[h] = jnp.broadcast_to(grown[:, h : h + 1], (tokens, width))
        fall_ref[h] = jnp.broadcast_to(fallen[:, h : h + 1], (tokens, width))
    ep_row = ep_ref[...].astype(F32)
    ep_col = jnp.broadcast_to(jnp.broadcast_to(ep_row, (8, tokens)).T[:, 0:1], (tokens, width))
    epc_ref[...] = ep_col
    first_id = ep_row[:, 0:1]
    last_id = ep_row[:, tokens - 1 : tokens]
    wide = jnp.concatenate([ep_col] * (tokens // width), axis=1)
    below = lax.broadcasted_iota(jnp.int32, (tokens, tokens), 0) >= lax.broadcasted_iota(
        jnp.int32, (tokens, tokens), 1
    )
    allow_ref[...] = jnp.where(below & (wide == ep_row), 0.0, BLOCKED)
    half = lax.broadcasted_iota(jnp.int32, (8, width), 1) < width // 2
    ids_ref[...] = jnp.where(half, first_id, last_id)

    beside = jnp.minimum(s, 1) + jnp.minimum(nseq - 1 - s, 1)
    across = jnp.minimum(z, 1) + jnp.minimum(groups - 1 - z, 1)
    pl.semaphore_wait(barrier, GROUP - 1 + nhead - 1 + beside + across)

    def remote(src, dst, send, recv, device):
        return pltpu.make_async_remote_copy(
            src_ref=src, dst_ref=dst, send_sem=send, recv_sem=recv, device_id=device, device_id_type=MESH
        )

    def ids_after():
        return remote(ids_ref, prev_ref, id_send.at[0], id_recv.at[0], {"seq": s + 1})

    def ids_before():
        return remote(ids_ref, next_ref, id_send.at[1], id_recv.at[1], {"seq": s - 1})

    @pl.when(s < nseq - 1)
    def _():
        ids_after().start()

    @pl.when(s > 0)
    def _():
        ids_before().start()

    @pl.when(s == 0)
    def _():
        prev_ref[...] = jnp.full_like(prev_ref, -1.0)

    @pl.when(s == nseq - 1)
    def _():
        next_ref[...] = jnp.full_like(next_ref, -1.0)

    @pl.when(s < nseq - 1)
    def _():
        ids_after().wait_send()
        ids_before().wait_recv()

    @pl.when(s > 0)
    def _():
        ids_before().wait_send()
        ids_after().wait_recv()

    prev_id = prev_ref[0:1, width - 1 : width]
    next_id = next_ref[0:1, 0:1]
    passed = jnp.broadcast_to(jnp.exp(total), (total.shape[0], width))
    keep_ref[0] = jnp.where(prev_id == last_id, passed, 0.0)
    keep_ref[1] = jnp.where(next_id == first_id, passed, 0.0)

    def up_copy(local, group, send, recv, position, i):
        return remote(
            local.at[position * owned + i], group.at[c, i], send.at[position, i], recv.at[c, i], member(position)
        )

    def up_wait(local, group, send, recv, position, i):
        remote(
            local.at[position * owned + i], group.at[position, i], send.at[position, i], recv.at[position, i],
            member(position),
        ).wait()

    def down_copy(leave, state, send, recv, position, i):
        return remote(
            leave.at[position, i], state.at[c * owned + i], send.at[position, i], recv.at[c, i], member(position)
        )

    def down_wait(leave, state, send, recv, position, i):
        remote(
            leave.at[position, i], state.at[position * owned + i], send.at[position, i], recv.at[position, i],
            member(position),
        ).wait()

    def local_states(i, _):
        for d in (1, 2, 3, 0):
            position = other(d)
            h = position * owned + i
            weight = jnp.where(epc_ref[...] == last_id, fall_ref[h], 0.0)
            decayed = (k_ref[h].astype(F32) * weight).astype(BF16)
            value = product(decayed, v_ref[h], 0, 0)
            factor = jnp.broadcast_to(keep_ref[0, pl.ds(h, 1), :], (8, width))
            if d == 0:
                group_ref[c, i, 0:width] = value
                group_ref[c, i, width:] = factor
            else:
                local_ref[h, 0:width] = value
                local_ref[h, width:] = factor
                up_copy(local_ref, group_ref, up_send, up_recv, position, i).start()
        return 0

    lax.fori_loop(0, owned, local_states, 0)

    def scan_owned(i, order, begin, has_before, has_after, local, group, chain, leave, enter, state, sems, step):
        usend, urecv, csend, crecv, dsend, drecv = sems

        for d in range(1, GROUP):
            up_wait(local, group, usend, urecv, other(d), i)

        def onward():
            return remote(enter.at[i], chain.at[i], csend.at[i], crecv.at[i], {"seq": s + step})

        def arrival():
            return remote(enter.at[i], chain.at[i], csend.at[i], crecv.at[i], {"seq": s - step})

        inner = None
        factors = None
        for j in order:
            leave_factor = group[j, i, width : width + 1, :]
            if inner is None:
                inner = group[j, i, 0:width]
                factors = leave_factor
            else:
                inner = inner * leave_factor + group[j, i, 0:width]
                factors = factors * leave_factor

        @pl.when(has_before)
        def _():
            arrival().wait_recv()

        @pl.when(jnp.logical_not(has_before))
        def _():
            chain[i] = jnp.zeros((width, width), F32)

        enter[i] = inner + factors * chain[i]

        @pl.when(has_after)
        def _():
            onward().start()

        carried = chain[i]
        for j in order:
            leave[j, i] = carried
            carried = carried * group[j, i, width : width + 1, :] + group[j, i, 0:width]
        for d in range(1, GROUP):
            down_copy(leave, state, dsend, drecv, other(d), i).start()
        state[c * owned + i] = leave[c, i]

        @pl.when(has_after)
        def _():
            onward().wait_send()

    def forward_part(i, _):
        for position in range(GROUP):
            h = position * owned + i
            runc = jnp.concatenate([runc_ref[h]] * (tokens // width), axis=1)
            decay = jnp.exp(runc - run_ref[pl.ds(h, 1), :] + allow_ref[...])
            decay_ref[h] = decay
            score = (product(q_ref[h], k_ref[h], 1, 1) * decay).astype(BF16)
            score_ref[h] = score
            att_ref[h] = product(score, v_ref[h], 1, 0)
        scan_owned(
            i, range(GROUP), 0, z > 0, z < groups - 1,
            local_ref, group_ref, chain_ref, leave_ref, enter_ref, state_ref,
            (up_send, up_recv, chain_send, chain_recv, down_send, down_recv), GROUP,
        )
        return 0

    lax.fori_loop(0, owned, forward_part, 0)

    sums_ref[...] = jnp.zeros_like(sums_ref)

    def attend(i, _):
        for d in range(1, GROUP):
            down_wait(leave_ref, state_ref, down_send, down_recv, other(d), i)
        squares = sums_ref[0]
        crosses = sums_ref[1]
        for position in range(GROUP):
            h = position * owned + i
            carried = jnp.where(epc_ref[...] == prev_id, grow_ref[h], 0.0)
            low = state_ref[h].astype(BF16)
            att = att_ref[h] + product(q_ref[h], low, 1, 0) * carried
            att_ref[h] = att
            squares = squares + att * att
            crosses = crosses + go_ref[h].astype(F32) * att
        sums_ref[0] = squares
        sums_ref[1] = crosses
        return 0

    lax.fori_loop(0, owned, attend, 0)
    square = jnp.sum(sums_ref[0], axis=1, keepdims=True)
    cross = jnp.sum(sums_ref[1], axis=1, keepdims=True)
    first_half = lax.broadcasted_iota(jnp.int32, (tokens, width), 1) < width // 2
    stat_ref[...] = jnp.where(first_half, square, cross)

    def stat_copy(d, slot):
        return remote(
            stat_ref, other_ref.at[slot], stat_send.at[d - 1], stat_recv.at[slot], {"head": lax.rem(hd + d, nhead)}
        )

    for d in range(1, nhead):
        stat_copy(d, d - 1).start()
    for d in range(1, nhead):
        stat_copy(d, d - 1).wait()
    summed = stat_ref[...]
    for d in range(1, nhead):
        summed = summed + other_ref[d - 1]
    square = summed[:, 0:1]
    cross = summed[:, width // 2 : width // 2 + 1]
    mean_square = square / features + EPSILON
    inverse = lax.rsqrt(mean_square)
    norm_ref[...] = jnp.broadcast_to(inverse, (tokens, width))
    corr_ref[...] = jnp.broadcast_to(cross / (features * mean_square), (tokens, width))

    def back_local(i, _):
        for d in (1, 2, 3, 0):
            position = other(d)
            h = position * owned + i
            att = att_ref[h]
            normed_ref[h] = (att * norm_ref[...]).astype(BF16)
            grad = ((go_ref[h].astype(F32) - att * corr_ref[...]) * norm_ref[...]).astype(BF16)
            gattn_ref[h] = grad
            weight = jnp.where(epc_ref[...] == first_id, grow_ref[h], 0.0)
            decayed = (q_ref[h].astype(F32) * weight).astype(BF16)
            value = product(decayed, grad, 0, 0)
            factor = jnp.broadcast_to(keep_ref[1, pl.ds(h, 1), :], (8, width))
            if d == 0:
                bgroup_ref[c, i, 0:width] = value
                bgroup_ref[c, i, width:] = factor
            else:
                blocal_ref[h, 0:width] = value
                blocal_ref[h, width:] = factor
                up_copy(blocal_ref, bgroup_ref, bup_send, bup_recv, position, i).start()
        return 0

    lax.fori_loop(0, owned, back_local, 0)

    def backward_part(i, _):
        for position in range(GROUP):
            h = position * owned + i
            grad = gattn_ref[h]
            grad_score = (product(grad, v_ref[h], 1, 1) * decay_ref[h]).astype(BF16)
            carried = jnp.where(epc_ref[...] == prev_id, grow_ref[h], 0.0)
            low = state_ref[h].astype(BF16)
            gq_ref[h] = (
                product(grad_score, k_ref[h], 1, 0) + product(grad, low, 1, 1) * carried
            ).astype(BF16)
            kin_ref[h] = product(grad_score, q_ref[h], 0, 0)
            vin_ref[h] = product(score_ref[h], grad, 0, 0)
        scan_owned(
            i, range(GROUP - 1, -1, -1), 0, z < groups - 1, z > 0,
            blocal_ref, bgroup_ref, bchain_ref, bleave_ref, benter_ref, bstate_ref,
            (bup_send, bup_recv, bchain_send, bchain_recv, bdown_send, bdown_recv), -GROUP,
        )
        return 0

    lax.fori_loop(0, owned, backward_part, 0)

    def finish(i, _):
        for d in range(1, GROUP):
            down_wait(bleave_ref, bstate_ref, bdown_send, bdown_recv, other(d), i)
        for position in range(GROUP):
            h = position * owned + i
            trailing = jnp.where(epc_ref[...] == next_id, fall_ref[h], 0.0)
            low = bstate_ref[h].astype(BF16)
            gk_ref[h] = (kin_ref[h] + product(v_ref[h], low, 1, 1) * trailing).astype(BF16)
            gv_ref[h] = (vin_ref[h] + product(k_ref[h], low, 1, 0) * trailing).astype(BF16)
        return 0

    lax.fori_loop(0, owned, finish, 0)


def per_device(nseq, nhead, query_rows, key_rows, value_rows, log_gate, episode, grad_out):
    heads, tokens, width = query_rows.shape
    owned = heads // GROUP
    padded = -(-heads // 8) * 8
    if padded != heads:
        log_gate = jnp.pad(log_gate, ((0, padded - heads), (0, 0)))
    vmem = pl.BlockSpec(memory_space=pltpu.VMEM)
    rows = jax.ShapeDtypeStruct(query_rows.shape, BF16)
    block = (heads, tokens, width)
    state_set = [
        pltpu.VMEM((heads, width + 8, width), F32),
        pltpu.VMEM((GROUP, owned, width + 8, width), F32),
        pltpu.VMEM((owned, width, width), F32),
        pltpu.VMEM((GROUP, owned, width, width), F32),
        pltpu.VMEM((owned, width, width), F32),
        pltpu.VMEM((heads, width, width), F32),
    ]
    sem_set = [
        pltpu.SemaphoreType.DMA((GROUP, owned)),
        pltpu.SemaphoreType.DMA((GROUP, owned)),
        pltpu.SemaphoreType.DMA((owned,)),
        pltpu.SemaphoreType.DMA((owned,)),
        pltpu.SemaphoreType.DMA((GROUP, owned)),
        pltpu.SemaphoreType.DMA((GROUP, owned)),
    ]
    others = max(nhead - 1, 1)
    return pl.pallas_call(
        functools.partial(kernel, nseq, nhead, float(heads * nhead * width)),
        out_shape=[rows] * 4,
        in_specs=[vmem] * 6,
        out_specs=[vmem] * 4,
        scratch_shapes=[
            pltpu.VMEM((padded, tokens), F32),
            pltpu.VMEM(block, F32),
            pltpu.VMEM(block, F32),
            pltpu.VMEM(block, F32),
            pltpu.VMEM((2, padded, width), F32),
            pltpu.VMEM((tokens, tokens), F32),
            pltpu.VMEM((tokens, width), F32),
            pltpu.VMEM((heads, tokens, tokens), F32),
            pltpu.VMEM((heads, tokens, tokens), BF16),
            pltpu.VMEM(block, F32),
            pltpu.VMEM(block, BF16),
            pltpu.VMEM(block, F32),
            pltpu.VMEM(block, F32),
            pltpu.VMEM((2, tokens, width), F32),
            pltpu.VMEM((tokens, width), F32),
            pltpu.VMEM((others, tokens, width), F32),
            pltpu.VMEM((tokens, width), F32),
            pltpu.VMEM((tokens, width), F32),
            pltpu.VMEM((8, width), F32),
            pltpu.VMEM((8, width), F32),
            pltpu.VMEM((8, width), F32),
            *state_set,
            *state_set,
            pltpu.SemaphoreType.DMA((2,)),
            pltpu.SemaphoreType.DMA((2,)),
            pltpu.SemaphoreType.DMA((others,)),
            pltpu.SemaphoreType.DMA((others,)),
            *sem_set,
            *sem_set,
        ],
        compiler_params=pltpu.CompilerParams(
            collective_id=0, has_side_effects=True, vmem_limit_bytes=56 * MIB
        ),
        cost_estimate=pl.CostEstimate(
            flops=heads * tokens * tokens * width * 18, bytes_accessed=heads * tokens * width * 16,
            transcendentals=heads * tokens * tokens,
        ),
    )(query_rows, key_rows, value_rows, log_gate, episode.reshape(1, tokens), grad_out)


def solution(mesh):
    rows = P("head", "seq", None)
    return jax.shard_map(
        functools.partial(per_device, mesh.shape["seq"], mesh.shape["head"]),
        mesh=mesh,
        in_specs=(rows, rows, rows, P("head", "seq"), P("seq"), rows),
        out_specs=(rows, rows, rows, rows),
        check_vma=False,
    )
```

time: 286 us -> 82.5 us (0.29)
  waiting for transfers between devices: 150 us -> 0 us
  Pallas kernels: 0 us -> 75 us
  starting transfers between devices: 74.3 us -> 0 us
  matrix products: 20.1 us -> 0 us
  other arithmetic: 17.1 us -> 0 us
  between operations: 12.6 us -> 0.65 us
    ppermute x22 -> x0, waiting for transfers between devices: 150 us -> none  [passed_along(): return lax.ppermute(block, axis, route)]
    pallas_call x0 -> x1, Pallas kernels: none -> 75 us  [per_device(): pl.pallas_call(functools.partial(kernel, nseq, nhead, float(heads * nhead...]
    ppermute x22 -> x0, starting transfers between devices: 74.3 us -> none  [passed_along(): return lax.ppermute(block, axis, route)]
    dot_general x12 -> x0, matrix products: 20.1 us -> none  [the longest x1 2.91 us: per_device(): jnp.einsum('hncd,hnsd->hncs', queries, keyset, preferred_element_type=jnp...]
    select_n x6 -> x0, other arithmetic: 8.58 us -> none  [the longest x2 4.52 us: reverse_merge_pass(): joined_state = jnp.where(empty_late, early_state, late_state + carried)]
    convert_element_type x3 -> x0, other arithmetic: 5.46 us -> none  [the longest x1 3.43 us: per_device(): grad_attn = ((cotangent_wide - attention * (crossed / (features * root_me...]
    unnamed x26 -> x10, local copies, waits for them, and re-layouts: 5.74 us -> 6.56 us
  transfers between devices with their start and end apart: 22 -> 0, of which waited for: 11 -> 0; matrix products, arithmetic and copies ran while one was open for 6% -> 0% of each run, Pallas kernels for 0% -> 0%
where the time goes in v1:
time: 82.5 us; the launch traced here: 82.2 us
  Pallas kernels  75 us (91%)
  local copies, waits for them, and re-layouts  6.56 us (8%)
    pallas_call x1, Pallas kernels, per_device(): pl.pallas_call(functools.partial(kernel, nseq, nhead, float(heads * nhead...  75 us
    unnamed x10, local copies, waits for them, and re-layouts  6.56 us

profile of v1, /device:TPU:0, one launch (start us, length us, event | category | flops | bytes accessed | tf_op | source)
XLA Modules:
  0.0 82.2 jit_solution(1045801724672435295)
XLA Ops:
  0.6 75.0 %shard_map.93 = (bf16[16,256,128]{2,1,0:T(8,128)(2,1)}, bf16[16,256,128]{2,1,0:T(8,128)(2,1)}, bf16[16,256,128]{2,1,0:T(8,128)(2,1)}, bf16[16,256,128]{2,1,0:T(8,128)(2,1)}) custom-call(bf16[16,256,128]{2,1,0:T(8,128)(2,1)} %q_ref.1, bf16[16,256,128]{2,1,0:T(8,128)(2,1)} %k_ref.1, bf16[16,256,128]{2,1,0:T(8,128)(2,1)} %v_ref.1, f32[16,256]{1,0:T(8,128)} %gate_ref.1, ...), custom_call_target="tpu_custom_call" | custom-call | flops 2415919104 | bytes 8388608 | tf_op jit(solution)/shard_map/pallas_call | solution.py:388
  75.6 0.0 copy-start.2
  75.6 2.4 %copy.14 = bf16[16,256,128]{2,1,0:T(8,128)(2,1)} copy(bf16[16,256,128]{2,1,0:T(8,128)(2,1)} %get-tuple-element.8) | data formatting | bytes 2097152
  78.0 0.0 copy-done.2
  78.0 0.0 copy-start.1
  78.0 1.0 %copy.15 = bf16[16,256,128]{2,1,0:T(8,128)(2,1)} copy(bf16[16,256,128]{2,1,0:T(8,128)(2,1)S(1)} %copy-done.2) | data formatting | bytes 2097152
  79.0 0.6 copy-done.1
  79.6 0.0 copy-start
  79.6 1.0 %copy.16 = bf16[16,256,128]{2,1,0:T(8,128)(2,1)} copy(bf16[16,256,128]{2,1,0:T(8,128)(2,1)S(1)} %copy-done.1) | data formatting | bytes 2097152
  80.6 0.6 copy-done
  81.2 1.0 %copy.17 = bf16[16,256,128]{2,1,0:T(8,128)(2,1)} copy(bf16[16,256,128]{2,1,0:T(8,128)(2,1)S(1)} %copy-done) | data formatting | bytes 2097152
Async XLA Ops:
  75.6 2.4 %copy-start.2 = (bf16[16,256,128]{2,1,0:T(8,128)(2,1)S(1)}, bf16[16,256,128]{2,1,0:T(8,128)(2,1)}, u32[]{:S(2)}) copy-start(bf16[16,256,128]{2,1,0:T(8,128)(2,1)} %get-tuple-element.9) | copy-start | bytes 3145732
  78.0 1.6 %copy-start.1 = (bf16[16,256,128]{2,1,0:T(8,128)(2,1)S(1)}, bf16[16,256,128]{2,1,0:T(8,128)(2,1)}, u32[]{:S(2)}) copy-start(bf16[16,256,128]{2,1,0:T(8,128)(2,1)} %get-tuple-element.10) | copy-start | bytes 3145732
  79.6 1.6 %copy-start = (bf16[16,256,128]{2,1,0:T(8,128)(2,1)S(1)}, bf16[16,256,128]{2,1,0:T(8,128)(2,1)}, u32[]{:S(2)}) copy-start(bf16[16,256,128]{2,1,0:T(8,128)(2,1)} %get-tuple-element.11) | copy-start | bytes 3145732

commit v2 on v1

v2 whole, which is shorter than its diff:
```python
import functools

import jax
import jax.numpy as jnp
from jax import lax
from jax.experimental import pallas as pl
from jax.experimental.pallas import tpu as pltpu
from jax.sharding import PartitionSpec as P

EPSILON = 1e-06
GROUP = 4
REACH_MAX = 16
BLOCKED = -1e30
MIB = 1 << 20
F32 = jnp.float32
BF16 = jnp.bfloat16
MESH = pl.DeviceIdType.MESH


def product(a, b, over_a, over_b):
    return lax.dot_general(a, b, (((over_a,), (over_b,)), ((), ())), preferred_element_type=F32)


def kernel(
    nseq, nhead, features,
    q_in, k_in, v_in, gate_ref, ep_ref, go_in,
    normed_out, gq_out, gk_out, gv_out,
    q_ref, k_ref, v_ref, go_ref, normed_ref, gq_ref, gk_ref, gv_ref,
    run_ref, runc_ref, grow_ref, fall_ref, pass_ref, allow_ref, epc_ref, decay_ref, score_ref,
    att_ref, gattn_ref, kin_ref, vin_ref, sums_ref, stat_ref, other_ref, norm_ref, corr_ref,
    ids_ref, prev_ref, next_ref,
    local_ref, group_ref, chain_ref, leave_ref, enter_ref, state_ref,
    blocal_ref, bgroup_ref, bchain_ref, bleave_ref, benter_ref, bstate_ref,
    in_sem, out_sem, gk_sem, gv_sem, id_send, id_recv, stat_send, stat_recv,
    up_send, up_recv, chain_send, chain_recv, down_send, down_recv,
    bup_send, bup_recv, bchain_send, bchain_recv, bdown_send, bdown_recv,
):
    heads, tokens, width = q_ref.shape
    owned = heads // GROUP
    groups = nseq // GROUP
    reach = chain_ref.shape[0]
    s = lax.axis_index("seq")
    hd = lax.axis_index("head")
    c = lax.rem(s, GROUP)
    z = s // GROUP
    base = s - c

    def member(position):
        return {"seq": base + position}

    def other(distance):
        return lax.rem(c + distance, GROUP)

    loads = [
        pltpu.make_async_copy(src, dst, in_sem.at[n])
        for n, (src, dst) in enumerate(((k_in, k_ref), (v_in, v_ref), (q_in, q_ref), (go_in, go_ref)))
    ]
    for load in loads:
        load.start()

    barrier = pltpu.get_barrier_semaphore()

    def greet(device):
        pl.semaphore_signal(barrier, inc=1, device_id=device, device_id_type=MESH)

    for d in range(1, GROUP):
        greet(member(other(d)))
    for d in range(1, nhead):
        greet({"head": lax.rem(hd + d, nhead)})

    @pl.when(s > 0)
    def _():
        greet({"seq": s - 1})

    @pl.when(s < nseq - 1)
    def _():
        greet({"seq": s + 1})

    for d in range(1, reach + 1):

        @pl.when(z >= d)
        def _():
            greet({"seq": s - GROUP * d})

        @pl.when(z < groups - d)
        def _():
            greet({"seq": s + GROUP * d})

    lane = lax.broadcasted_iota(jnp.int32, gate_ref.shape, 1)
    run = gate_ref[...]
    step = 1
    while step < tokens:
        run = run + jnp.where(lane >= step, pltpu.roll(run, step, 1), 0.0)
        step *= 2
    run_ref[...] = run
    total = run[:, tokens - 1 : tokens]
    fallen = jnp.exp(total - run).T
    for h in range(heads):
        fall_ref[h] = jnp.broadcast_to(fallen[:, h : h + 1], (tokens, width))
    pass_ref[...] = jnp.broadcast_to(jnp.exp(total), (total.shape[0], width))
    ep_row = ep_ref[...].astype(F32)
    ep_col = jnp.broadcast_to(jnp.broadcast_to(ep_row, (8, tokens)).T[:, 0:1], (tokens, width))
    epc_ref[...] = ep_col
    first_id = ep_row[:, 0:1]
    last_id = ep_row[:, tokens - 1 : tokens]
    half = lax.broadcasted_iota(jnp.int32, (8, width), 1) < width // 2
    ids_ref[...] = jnp.where(half, first_id, last_id)
    row = lax.broadcasted_iota(jnp.int32, (8, width), 0)
    id_rows = jnp.where(row == 1, last_id, first_id)
    loads[0].wait()
    loads[1].wait()

    def local_state(i, position, target, at):
        h = position * owned + i
        weight = jnp.where(epc_ref[...] == last_id, fall_ref[h], 0.0)
        decayed = (k_ref[h].astype(F32) * weight).astype(BF16)
        target[*at, 0:width] = product(decayed, v_ref[h], 0, 0)
        target[*at, width:] = jnp.where(row == 0, pass_ref[pl.ds(h, 1), :], id_rows)

    def local_states(i):
        for d in (1, 2, 3):
            local_state(i, other(d), local_ref, (other(d) * owned + i,))
        local_state(i, c, group_ref, (c, i))

    local_states(0)

    beside = jnp.minimum(s, 1) + jnp.minimum(nseq - 1 - s, 1)
    across = jnp.minimum(z, reach) + jnp.minimum(groups - 1 - z, reach)
    pl.semaphore_wait(barrier, GROUP - 1 + nhead - 1 + beside + across)

    def remote(src, dst, send, recv, device):
        return pltpu.make_async_remote_copy(
            src_ref=src, dst_ref=dst, send_sem=send, recv_sem=recv, device_id=device, device_id_type=MESH
        )

    def ids_after():
        return remote(ids_ref, prev_ref, id_send.at[0], id_recv.at[0], {"seq": s + 1})

    def ids_before():
        return remote(ids_ref, next_ref, id_send.at[1], id_recv.at[1], {"seq": s - 1})

    def up_copy(local, group, send, recv, position, i):
        return remote(
            local.at[position * owned + i], group.at[c, i], send.at[position, i], recv.at[c, i], member(position)
        )

    def up_arrival(local, group, send, recv, position, i):
        return remote(
            local.at[position * owned + i], group.at[position, i], send.at[position, i], recv.at[position, i],
            member(position),
        )

    def down_copy(leave, state, send, recv, position, i):
        return remote(
            leave.at[position, i], state.at[c * owned + i], send.at[position, i], recv.at[c, i], member(position)
        )

    def down_arrival(leave, state, send, recv, position, i):
        return remote(
            leave.at[position, i], state.at[position * owned + i], send.at[position, i], recv.at[position, i],
            member(position),
        )

    forward_set = (
        local_ref, group_ref, chain_ref, leave_ref, enter_ref, state_ref,
        up_send, up_recv, chain_send, chain_recv, down_send, down_recv,
    )
    backward_set = (
        blocal_ref, bgroup_ref, bchain_ref, bleave_ref, benter_ref, bstate_ref,
        bup_send, bup_recv, bchain_send, bchain_recv, bdown_send, bdown_recv,
    )

    def send_local(i, buffers):
        local, group, _, _, _, _, usend, urecv = buffers[:8]
        for d in (1, 2, 3):
            up_copy(local, group, usend, urecv, other(d), i).start()

    send_local(0, forward_set)

    @pl.when(s < nseq - 1)
    def _():
        ids_after().start()

    @pl.when(s > 0)
    def _():
        ids_before().start()

    def more_states(i, _):
        local_states(i)
        send_local(i, forward_set)
        return 0

    lax.fori_loop(1, owned, more_states, 0)

    columns = run.T
    grown = jnp.exp(run).T
    for h in range(heads):
        runc_ref[h] = jnp.broadcast_to(columns[:, h : h + 1], (tokens, width))
        grow_ref[h] = jnp.broadcast_to(grown[:, h : h + 1], (tokens, width))
    wide = jnp.concatenate([epc_ref[...]] * (tokens // width), axis=1)
    below = lax.broadcasted_iota(jnp.int32, (tokens, tokens), 0) >= lax.broadcasted_iota(
        jnp.int32, (tokens, tokens), 1
    )
    allow_ref[...] = jnp.where(below & (wide == ep_row), 0.0, BLOCKED)

    def chain_copy(buffers, i, distance, sign):
        _, _, chain, _, enter, _, _, _, csend, crecv, _, _ = buffers
        return remote(
            enter.at[i], chain.at[distance - 1, i], csend.at[distance - 1, i], crecv.at[distance - 1, i],
            {"seq": s + sign * GROUP * distance},
        )

    def exists(distance, sign):
        return z < groups - distance if sign > 0 else z >= distance

    def send_total(i, sign, buffers):
        local, group, chain, leave, enter, state, usend, urecv, csend, crecv, dsend, drecv = buffers
        id_row = width + 1 if sign > 0 else width + 2
        for d in range(1, GROUP):
            up_arrival(local, group, usend, urecv, other(d), i).wait_recv()
        total_state = None
        for j in range(GROUP)[::sign]:
            factor = group[j, i, width : width + 1, :]
            mark = group[j, i, id_row : id_row + 1, :]
            if total_state is None:
                total_state = group[j, i, 0:width]
                factors = factor
            else:
                total_state = total_state * jnp.where(mark == before, factor, 0.0) + group[j, i, 0:width]
                factors = factors * factor
            before = mark
        enter[i, 0:width] = total_state
        enter[i, width:] = jnp.where(row == 0, factors, before)
        for d in range(1, reach + 1):

            @pl.when(exists(d, sign))
            def _():
                chain_copy(buffers, i, d, sign).start()

    def send_entering(i, sign, buffers):
        local, group, chain, leave, enter, state, usend, urecv, csend, crecv, dsend, drecv = buffers
        id_row = width + 1 if sign > 0 else width + 2
        for d in range(1, reach + 1):

            @pl.when(exists(d, -sign))
            def _():
                chain_copy(buffers, i, d, -sign).wait_recv()

            @pl.when(jnp.logical_not(exists(d, -sign)))
            def _():
                chain[d - 1, i] = jnp.zeros((width + 8, width), F32)

        carried = chain[reach - 1, i, 0:width]
        before = chain[reach - 1, i, width + 1 : width + 2, :]
        for d in range(reach - 1, 0, -1):
            mark = chain[d - 1, i, width + 1 : width + 2, :]
            factor = jnp.where(mark == before, chain[d - 1, i, width : width + 1, :], 0.0)
            carried = carried * factor + chain[d - 1, i, 0:width]
            before = mark
        for n, j in enumerate(range(GROUP)[::sign]):
            leave[j, i] = carried
            if n < GROUP - 1:
                mark = group[j, i, id_row : id_row + 1, :]
                factor = jnp.where(mark == before, group[j, i, width : width + 1, :], 0.0)
                carried = carried * factor + group[j, i, 0:width]
                before = mark
        for d in range(1, GROUP):
            down_copy(leave, state, dsend, drecv, other(d), i).start()
        state[c * owned + i] = leave[c, i]

    def state_arrival(i, buffers):
        _, _, _, leave, _, state, _, _, _, _, dsend, drecv = buffers
        for d in range(1, GROUP):
            down_arrival(leave, state, dsend, drecv, other(d), i).wait_recv()

    def settle(i, sign, buffers):
        local, group, _, leave, _, state, usend, urecv, _, _, dsend, drecv = buffers
        for d in range(1, GROUP):
            up_arrival(local, group, usend, urecv, other(d), i).wait_send()
            down_arrival(leave, state, dsend, drecv, other(d), i).wait_send()
        for d in range(1, reach + 1):

            @pl.when(exists(d, sign))
            def _():
                chain_copy(buffers, i, d, sign).wait_send()

    def scan(sign, buffers, part):
        part(0)

        def steps(i, _):
            send_total(i, sign, buffers)

            @pl.when(i < owned - 1)
            def _():
                part(i + 1)

            send_entering(i, sign, buffers)
            return 0

        lax.fori_loop(0, owned, steps, 0)

    def forward_part(i):
        for position in range(GROUP):
            h = position * owned + i
            runc = jnp.concatenate([runc_ref[h]] * (tokens // width), axis=1)
            decay = jnp.exp(runc - run_ref[pl.ds(h, 1), :] + allow_ref[...])
            decay_ref[h] = decay
            score = (product(q_ref[h], k_ref[h], 1, 1) * decay).astype(BF16)
            score_ref[h] = score
            att_ref[h] = product(score, v_ref[h], 1, 0)

    loads[2].wait()
    scan(1, forward_set, forward_part)

    @pl.when(s == 0)
    def _():
        prev_ref[...] = jnp.full_like(prev_ref, -1.0)

    @pl.when(s == nseq - 1)
    def _():
        next_ref[...] = jnp.full_like(next_ref, -1.0)

    @pl.when(s < nseq - 1)
    def _():
        ids_after().wait_send()
        ids_before().wait_recv()

    @pl.when(s > 0)
    def _():
        ids_before().wait_send()
        ids_after().wait_recv()

    prev_id = prev_ref[0:1, width - 1 : width]
    next_id = next_ref[0:1, 0:1]
    loads[3].wait()

    sums_ref[...] = jnp.zeros_like(sums_ref)

    def attend(i, _):
        state_arrival(i, forward_set)
        squares = sums_ref[0]
        crosses = sums_ref[1]
        for position in range(GROUP):
            h = position * owned + i
            carried = jnp.where(epc_ref[...] == prev_id, grow_ref[h], 0.0)
            low = state_ref[h].astype(BF16)
            att = att_ref[h] + product(q_ref[h], low, 1, 0) * carried
            att_ref[h] = att
            squares = squares + att * att
            crosses = crosses + go_ref[h].astype(F32) * att
        sums_ref[0] = squares
        sums_ref[1] = crosses
        return 0

    lax.fori_loop(0, owned, attend, 0)
    square = jnp.sum(sums_ref[0], axis=1, keepdims=True)
    cross = jnp.sum(sums_ref[1], axis=1, keepdims=True)
    first_half = lax.broadcasted_iota(jnp.int32, (tokens, width), 1) < width // 2
    stat_ref[...] = jnp.where(first_half, square, cross)

    def stat_copy(d, slot):
        return remote(
            stat_ref, other_ref.at[slot], stat_send.at[d - 1], stat_recv.at[slot], {"head": lax.rem(hd + d, nhead)}
        )

    for d in range(1, nhead):
        stat_copy(d, d - 1).start()
    for d in range(1, nhead):
        stat_copy(d, d - 1).wait()
    summed = stat_ref[...]
    for d in range(1, nhead):
        summed = summed + other_ref[d - 1]
    square = summed[:, 0:1]
    cross = summed[:, width // 2 : width // 2 + 1]
    mean_square = square / features + EPSILON
    inverse = lax.rsqrt(mean_square)
    norm_ref[...] = jnp.broadcast_to(inverse, (tokens, width))
    corr_ref[...] = jnp.broadcast_to(cross / (features * mean_square), (tokens, width))

    def back_local(i, _):
        for d in (1, 2, 3, 0):
            position = other(d)
            h = position * owned + i
            att = att_ref[h]
            normed_ref[h] = (att * norm_ref[...]).astype(BF16)
            grad = ((go_ref[h].astype(F32) - att * corr_ref[...]) * norm_ref[...]).astype(BF16)
            gattn_ref[h] = grad
            weight = jnp.where(epc_ref[...] == first_id, grow_ref[h], 0.0)
            decayed = (q_ref[h].astype(F32) * weight).astype(BF16)
            value = product(decayed, grad, 0, 0)
            below_rows = jnp.where(row == 0, pass_ref[pl.ds(h, 1), :], id_rows)
            if d == 0:
                bgroup_ref[c, i, 0:width] = value
                bgroup_ref[c, i, width:] = below_rows
            else:
                blocal_ref[h, 0:width] = value
                blocal_ref[h, width:] = below_rows
                up_copy(blocal_ref, bgroup_ref, bup_send, bup_recv, position, i).start()
        return 0

    lax.fori_loop(0, owned, back_local, 0)
    normed_store = pltpu.make_async_copy(normed_ref, normed_out, out_sem.at[0])
    normed_store.start()

    def backward_part(i):
        for position in range(GROUP):
            h = position * owned + i
            grad = gattn_ref[h]
            grad_score = (product(grad, v_ref[h], 1, 1) * decay_ref[h]).astype(BF16)
            carried = jnp.where(epc_ref[...] == prev_id, grow_ref[h], 0.0)
            low = state_ref[h].astype(BF16)
            gq_ref[h] = (
                product(grad_score, k_ref[h], 1, 0) + product(grad, low, 1, 1) * carried
            ).astype(BF16)
            kin_ref[h] = product(grad_score, q_ref[h], 0, 0)
            vin_ref[h] = product(score_ref[h], grad, 0, 0)

    scan(-1, backward_set, backward_part)
    gq_store = pltpu.make_async_copy(gq_ref, gq_out, out_sem.at[1])
    gq_store.start()

    def stores(h):
        return (
            pltpu.make_async_copy(gk_ref.at[h], gk_out.at[h], gk_sem.at[h]),
            pltpu.make_async_copy(gv_ref.at[h], gv_out.at[h], gv_sem.at[h]),
        )

    def finish(i, _):
        state_arrival(i, backward_set)
        for position in range(GROUP):
            h = position * owned + i
            trailing = jnp.where(epc_ref[...] == next_id, fall_ref[h], 0.0)
            low = bstate_ref[h].astype(BF16)
            gk_ref[h] = (kin_ref[h] + product(v_ref[h], low, 1, 1) * trailing).astype(BF16)
            gv_ref[h] = (vin_ref[h] + product(k_ref[h], low, 1, 0) * trailing).astype(BF16)
            for store in stores(h):
                store.start()
        return 0

    lax.fori_loop(0, owned, finish, 0)

    def settle_all(i, _):
        settle(i, 1, forward_set)
        settle(i, -1, backward_set)
        for position in range(GROUP):
            for store in stores(position * owned + i):
                store.wait()
        return 0

    lax.fori_loop(0, owned, settle_all, 0)
    normed_store.wait()
    gq_store.wait()


def hand_over(*refs):
    sources, targets, held, in_sem, out_sem = refs[:4], refs[4:8], refs[8], refs[9], refs[10]
    pairs = []
    for n in range(len(sources)):
        heads = sources[n].shape[0]
        for part in range(2):
            rows = pl.ds(part * heads // 2, heads // 2)
            slot = held.at[n, rows]
            pairs.append((
                pltpu.make_async_copy(sources[n].at[rows], slot, in_sem.at[n, part]),
                pltpu.make_async_copy(slot, targets[n].at[rows], out_sem.at[n, part]),
            ))
    for load, _ in pairs:
        load.start()
    for load, store in pairs:
        load.wait()
        store.start()
    for _, store in pairs:
        store.wait()


def per_device(nseq, nhead, query_rows, key_rows, value_rows, log_gate, episode, grad_out):
    heads, tokens, width = query_rows.shape
    owned = heads // GROUP
    padded = -(-heads // 8) * 8
    if padded != heads:
        log_gate = jnp.pad(log_gate, ((0, padded - heads), (0, 0)))
    reach = -(-min(REACH_MAX, nseq // 2) // GROUP)
    vmem = pl.BlockSpec(memory_space=pltpu.VMEM)
    outside = pl.BlockSpec(memory_space=pl.ANY)
    rows = jax.ShapeDtypeStruct(query_rows.shape, BF16)
    block = (heads, tokens, width)
    state_set = [
        pltpu.VMEM((heads, width + 8, width), F32),
        pltpu.VMEM((GROUP, owned, width + 8, width), F32),
        pltpu.VMEM((reach, owned, width + 8, width), F32),
        pltpu.VMEM((GROUP, owned, width, width), F32),
        pltpu.VMEM((owned, width + 8, width), F32),
        pltpu.VMEM((heads, width, width), F32),
    ]
    sem_set = [
        pltpu.SemaphoreType.DMA((GROUP, owned)),
        pltpu.SemaphoreType.DMA((GROUP, owned)),
        pltpu.SemaphoreType.DMA((reach, owned)),
        pltpu.SemaphoreType.DMA((reach, owned)),
        pltpu.SemaphoreType.DMA((GROUP, owned)),
        pltpu.SemaphoreType.DMA((GROUP, owned)),
    ]
    others = max(nhead - 1, 1)
    results = pl.pallas_call(
        functools.partial(kernel, nseq, nhead, float(heads * nhead * width)),
        out_shape=[rows] * 4,
        in_specs=[outside, outside, outside, vmem, vmem, outside],
        out_specs=[outside] * 4,
        scratch_shapes=[
            *[pltpu.VMEM(block, BF16)] * 8,
            pltpu.VMEM((padded, tokens), F32),
            pltpu.VMEM(block, F32),
            pltpu.VMEM(block, F32),
            pltpu.VMEM(block, F32),
            pltpu.VMEM((padded, width), F32),
            pltpu.VMEM((tokens, tokens), F32),
            pltpu.VMEM((tokens, width), F32),
            pltpu.VMEM((heads, tokens, tokens), F32),
            pltpu.VMEM((heads, tokens, tokens), BF16),
            pltpu.VMEM(block, F32),
            pltpu.VMEM(block, BF16),
            pltpu.VMEM(block, F32),
            pltpu.VMEM(block, F32),
            pltpu.VMEM((2, tokens, width), F32),
            pltpu.VMEM((tokens, width), F32),
            pltpu.VMEM((others, tokens, width), F32),
            pltpu.VMEM((tokens, width), F32),
            pltpu.VMEM((tokens, width), F32),
            pltpu.VMEM((8, width), F32),
            pltpu.VMEM((8, width), F32),
            pltpu.VMEM((8, width), F32),
            *state_set,
            *state_set,
            pltpu.SemaphoreType.DMA((4,)),
            pltpu.SemaphoreType.DMA((2,)),
            pltpu.SemaphoreType.DMA((heads,)),
            pltpu.SemaphoreType.DMA((heads,)),
            pltpu.SemaphoreType.DMA((2,)),
            pltpu.SemaphoreType.DMA((2,)),
            pltpu.SemaphoreType.DMA((others,)),
            pltpu.SemaphoreType.DMA((others,)),
            *sem_set,
            *sem_set,
        ],
        compiler_params=pltpu.CompilerParams(
            collective_id=0, has_side_effects=True, vmem_limit_bytes=56 * MIB
        ),
        cost_estimate=pl.CostEstimate(
            flops=heads * tokens * tokens * width * 18, bytes_accessed=heads * tokens * width * 16,
            transcendentals=heads * tokens * tokens,
        ),
    )(query_rows, key_rows, value_rows, log_gate, episode.reshape(1, tokens), grad_out)
    return pl.pallas_call(
        hand_over,
        out_shape=[rows] * 4,
        in_specs=[outside] * 4,
        out_specs=[outside] * 4,
        scratch_shapes=[
            pltpu.VMEM((4, *block), BF16),
            pltpu.SemaphoreType.DMA((4, 2)),
            pltpu.SemaphoreType.DMA((4, 2)),
        ],
        compiler_params=pltpu.CompilerParams(vmem_limit_bytes=56 * MIB),
    )(*results)


def solution(mesh):
    rows = P("head", "seq", None)
    return jax.shard_map(
        functools.partial(per_device, mesh.shape["seq"], mesh.shape["head"]),
        mesh=mesh,
        in_specs=(rows, rows, rows, P("head", "seq"), P("seq"), rows),
        out_specs=(rows, rows, rows, rows),
        check_vma=False,
    )
```

time: 82.5 us -> 74 us (0.90)
  local copies, waits for them, and re-layouts: 6.56 us -> 0 us
  Pallas kernels: 75 us -> 73.1 us
    unnamed x10 -> x0, local copies, waits for them, and re-layouts: 6.56 us -> none
    pallas_call x1, Pallas kernels: 75 us -> 69.6 us  [per_device(): pl.pallas_call(functools.partial(kernel, nseq, nhead, float(heads * nhead...]
    pallas_call x0 -> x1, Pallas kernels: none -> 3.58 us  [per_device(): pl.pallas_call(hand_over, out_shape=[rows] * 4, in_specs=[outside] * 4, o...]
where the time goes in v2:
time: 74 us; the launch traced here: 73.8 us
  Pallas kernels  73.1 us (99%)
    pallas_call x1, Pallas kernels, per_device(): pl.pallas_call(functools.partial(kernel, nseq, nhead, float(heads * nhead...  69.6 us
    pallas_call x1, Pallas kernels, per_device(): pl.pallas_call(hand_over, out_shape=[rows] * 4, in_specs=[outside] * 4, o...  3.58 us

profile of v2, /device:TPU:0, one launch (start us, length us, event | category | flops | bytes accessed | tf_op | source)
XLA Modules:
  0.0 73.8 jit_solution(9253880346998218275)
XLA Ops:
  0.6 69.6 %shard_map.93 = (bf16[16,256,128]{2,1,0:T(8,128)(2,1)}, bf16[16,256,128]{2,1,0:T(8,128)(2,1)}, bf16[16,256,128]{2,1,0:T(8,128)(2,1)}, bf16[16,256,128]{2,1,0:T(8,128)(2,1)}) custom-call(bf16[16,256,128]{2,1,0:T(8,128)(2,1)} %q_in.1, bf16[16,256,128]{2,1,0:T(8,128)(2,1)} %k_in.1, bf16[16,256,128]{2,1,0:T(8,128)(2,1)} %v_in.1, f32[16,256]{1,0:T(8,128)} %gate_ref.1, ...), custom_call_target="tpu_custom_call" | custom-call | flops 2415919104 | bytes 8388608 | tf_op jit(solution)/shard_map/pallas_call | solution.py:504
  70.2 3.6 %shard_map.94 = (bf16[16,256,128]{2,1,0:T(8,128)(2,1)}, bf16[16,256,128]{2,1,0:T(8,128)(2,1)}, bf16[16,256,128]{2,1,0:T(8,128)(2,1)}, bf16[16,256,128]{2,1,0:T(8,128)(2,1)}) custom-call(bf16[16,256,128]{2,1,0:T(8,128)(2,1)} %get-tuple-element.8.refs_0_, bf16[16,256,128]{2,1,0:T(8,128)(2,1)} %get-tuple-element.9.refs_1_, ...), custom_call_target="tpu_custom_call" | custom-call | tf_op jit(solution)/shard_map/pallas_call | solution.py:553

commit v3 on v2

--- a/solution.py
+++ b/solution.py
@@ -9,7 +9,6 @@
 
 EPSILON = 1e-06
 GROUP = 4
-REACH_MAX = 16
 BLOCKED = -1e30
 MIB = 1 << 20
 F32 = jnp.float32
@@ -38,7 +37,7 @@
     heads, tokens, width = q_ref.shape
     owned = heads // GROUP
     groups = nseq // GROUP
-    reach = chain_ref.shape[0]
+    reach = 2
     s = lax.axis_index("seq")
     hd = lax.axis_index("head")
     c = lax.rem(s, GROUP)
@@ -203,15 +202,18 @@
     )
     allow_ref[...] = jnp.where(below & (wide == ep_row), 0.0, BLOCKED)
 
-    def chain_copy(buffers, i, distance, sign):
+    def chain_copy(buffers, i, slot, distance, sign):
         _, _, chain, _, enter, _, _, _, csend, crecv, _, _ = buffers
         return remote(
-            enter.at[i], chain.at[distance - 1, i], csend.at[distance - 1, i], crecv.at[distance - 1, i],
+            enter.at[i], chain.at[slot, i], csend.at[distance - 1, i], crecv.at[slot, i],
             {"seq": s + sign * GROUP * distance},
         )
 
-    def exists(distance, sign):
-        return z < groups - distance if sign > 0 else z >= distance
+    def place(sign):
+        return z if sign > 0 else groups - 1 - z
+
+    def latter(sign):
+        return lax.rem(place(sign), 2) == 1
 
     def send_total(i, sign, buffers):
         local, group, chain, leave, enter, state, usend, urecv, csend, crecv, dsend, drecv = buffers
@@ -231,32 +233,42 @@
             before = mark
         enter[i, 0:width] = total_state
         enter[i, width:] = jnp.where(row == 0, factors, before)
-        for d in range(1, reach + 1):
-
-            @pl.when(exists(d, sign))
-            def _():
-                chain_copy(buffers, i, d, sign).start()
+
+        @pl.when(jnp.logical_not(latter(sign)))
+        def _():
+            chain_copy(buffers, i, 1, 1, sign).start()
 
     def send_entering(i, sign, buffers):
         local, group, chain, leave, enter, state, usend, urecv, csend, crecv, dsend, drecv = buffers
         id_row = width + 1 if sign > 0 else width + 2
-        for d in range(1, reach + 1):
-
-            @pl.when(exists(d, -sign))
+
+        @pl.when(place(sign) < 2)
+        def _():
+            chain[0, i] = jnp.zeros((width + 8, width), F32)
+
+        @pl.when(place(sign) >= 2)
+        def _():
+            chain_copy(buffers, i, 0, 1, -sign).wait_recv()
+
+        @pl.when(latter(sign))
+        def _():
+            chain_copy(buffers, i, 1, 1, -sign).wait_recv()
+            mark = chain[1, i, width + 1 : width + 2, :]
+            factor = jnp.where(mark == chain[0, i, width + 1 : width + 2, :], chain[1, i, width : width + 1, :], 0.0)
+            entering = chain[0, i, 0:width] * factor + chain[1, i, 0:width]
+            chain[0, i, 0:width] = entering
+            chain[0, i, width:] = jnp.broadcast_to(mark, (8, width))
+            own = enter[i, width + 1 : width + 2, :]
+            factor = jnp.where(own == mark, enter[i, width : width + 1, :], 0.0)
+            enter[i, 0:width] = entering * factor + enter[i, 0:width]
+
+            @pl.when(place(sign) < groups - 1)
             def _():
-                chain_copy(buffers, i, d, -sign).wait_recv()
-
-            @pl.when(jnp.logical_not(exists(d, -sign)))
-            def _():
-                chain[d - 1, i] = jnp.zeros((width + 8, width), F32)
-
-        carried = chain[reach - 1, i, 0:width]
-        before = chain[reach - 1, i, width + 1 : width + 2, :]
-        for d in range(reach - 1, 0, -1):
-            mark = chain[d - 1, i, width + 1 : width + 2, :]
-            factor = jnp.where(mark == before, chain[d - 1, i, width : width + 1, :], 0.0)
-            carried = carried * factor + chain[d - 1, i, 0:width]
-            before = mark
+                chain_copy(buffers, i, 0, 1, sign).start()
+                chain_copy(buffers, i, 0, 2, sign).start()
+
+        carried = chain[0, i, 0:width]
+        before = chain[0, i, width + 1 : width + 2, :]
         for n, j in enumerate(range(GROUP)[::sign]):
             leave[j, i] = carried
             if n < GROUP - 1:
@@ -278,11 +290,14 @@
         for d in range(1, GROUP):
             up_arrival(local, group, usend, urecv, other(d), i).wait_send()
             down_arrival(leave, state, dsend, drecv, other(d), i).wait_send()
-        for d in range(1, reach + 1):
-
-            @pl.when(exists(d, sign))
-            def _():
-                chain_copy(buffers, i, d, sign).wait_send()
+
+        @pl.when(place(sign) < groups - 1)
+        def _():
+            chain_copy(buffers, i, 0, 1, sign).wait_send()
+
+        @pl.when(latter(sign) & (place(sign) < groups - 1))
+        def _():
+            chain_copy(buffers, i, 0, 2, sign).wait_send()
 
     def scan(sign, buffers, part):
         part(0)
@@ -479,7 +494,6 @@
     padded = -(-heads // 8) * 8
     if padded != heads:
         log_gate = jnp.pad(log_gate, ((0, padded - heads), (0, 0)))
-    reach = -(-min(REACH_MAX, nseq // 2) // GROUP)
     vmem = pl.BlockSpec(memory_space=pltpu.VMEM)
     outside = pl.BlockSpec(memory_space=pl.ANY)
     rows = jax.ShapeDtypeStruct(query_rows.shape, BF16)
@@ -487,7 +501,7 @@
     state_set = [
         pltpu.VMEM((heads, width + 8, width), F32),
         pltpu.VMEM((GROUP, owned, width + 8, width), F32),
-        pltpu.VMEM((reach, owned, width + 8, width), F32),
+        pltpu.VMEM((2, owned, width + 8, width), F32),
         pltpu.VMEM((GROUP, owned, width, width), F32),
         pltpu.VMEM((owned, width + 8, width), F32),
         pltpu.VMEM((heads, width, width), F32),
@@ -495,8 +509,8 @@
     sem_set = [
         pltpu.SemaphoreType.DMA((GROUP, owned)),
         pltpu.SemaphoreType.DMA((GROUP, owned)),
-        pltpu.SemaphoreType.DMA((reach, owned)),
-        pltpu.SemaphoreType.DMA((reach, owned)),
+        pltpu.SemaphoreType.DMA((2, owned)),
+        pltpu.SemaphoreType.DMA((2, owned)),
         pltpu.SemaphoreType.DMA((GROUP, owned)),
         pltpu.SemaphoreType.DMA((GROUP, owned)),
     ]

time: 74 us -> 69.6 us (0.941)
  Pallas kernels: 73.1 us -> 68.7 us
    pallas_call x1, Pallas kernels: 69.6 us -> 65.1 us  [per_device(): pl.pallas_call(functools.partial(kernel, nseq, nhead, float(heads * nhead...]
where the time goes in v3:
time: 69.6 us; the launch traced here: 69.3 us
  Pallas kernels  68.7 us (99%)
    pallas_call x1, Pallas kernels, per_device(): pl.pallas_call(functools.partial(kernel, nseq, nhead, float(heads * nhead...  65.1 us
    pallas_call x1, Pallas kernels, per_device(): pl.pallas_call(hand_over, out_shape=[rows] * 4, in_specs=[outside] * 4, o...  3.58 us

profile of v3, /device:TPU:0, one launch (start us, length us, event | category | flops | bytes accessed | tf_op | source)
XLA Modules:
  0.0 69.3 jit_solution(13456300867950098392)
XLA Ops:
  0.6 65.1 %shard_map.93 = (bf16[16,256,128]{2,1,0:T(8,128)(2,1)}, bf16[16,256,128]{2,1,0:T(8,128)(2,1)}, bf16[16,256,128]{2,1,0:T(8,128)(2,1)}, bf16[16,256,128]{2,1,0:T(8,128)(2,1)}) custom-call(bf16[16,256,128]{2,1,0:T(8,128)(2,1)} %q_in.1, bf16[16,256,128]{2,1,0:T(8,128)(2,1)} %k_in.1, bf16[16,256,128]{2,1,0:T(8,128)(2,1)} %v_in.1, f32[16,256]{1,0:T(8,128)} %gate_ref.1, ...), custom_call_target="tpu_custom_call" | custom-call | flops 2415919104 | bytes 8388608 | tf_op jit(solution)/shard_map/pallas_call | solution.py:518
  65.7 3.6 %shard_map.94 = (bf16[16,256,128]{2,1,0:T(8,128)(2,1)}, bf16[16,256,128]{2,1,0:T(8,128)(2,1)}, bf16[16,256,128]{2,1,0:T(8,128)(2,1)}, bf16[16,256,128]{2,1,0:T(8,128)(2,1)}) custom-call(bf16[16,256,128]{2,1,0:T(8,128)(2,1)} %get-tuple-element.8.refs_0_, bf16[16,256,128]{2,1,0:T(8,128)(2,1)} %get-tuple-element.9.refs_1_, ...), custom_call_target="tpu_custom_call" | custom-call | tf_op jit(solution)/shard_map/pallas_call | solution.py:567

commit v4 on v3

--- a/solution.py
+++ b/solution.py
@@ -238,34 +238,48 @@
         def _():
             chain_copy(buffers, i, 1, 1, sign).start()
 
+    def receive_state(i, sign, buffers):
+        chain = buffers[2]
+
+        @pl.when(place(sign) < 2)
+        def _():
+            chain[0, i] = jnp.zeros((width + 8, width), F32)
+
+        @pl.when(place(sign) >= 2)
+        def _():
+            chain_copy(buffers, i, 0, 1, -sign).wait_recv()
+
+    def join_pair(i, sign, buffers):
+        chain, enter = buffers[2], buffers[4]
+        receive_state(i, sign, buffers)
+        chain_copy(buffers, i, 1, 1, -sign).wait_recv()
+        mark = chain[1, i, width + 1 : width + 2, :]
+        factor = jnp.where(mark == chain[0, i, width + 1 : width + 2, :], chain[1, i, width : width + 1, :], 0.0)
+        entering = chain[0, i, 0:width] * factor + chain[1, i, 0:width]
+        chain[0, i, 0:width] = entering
+        chain[0, i, width:] = jnp.broadcast_to(mark, (8, width))
+        own = enter[i, width + 1 : width + 2, :]
+        factor = jnp.where(own == mark, enter[i, width : width + 1, :], 0.0)
+        enter[i, 0:width] = entering * factor + enter[i, 0:width]
+
+    def send_next(i, sign, buffers):
+        @pl.when(latter(sign) & (place(sign) < groups - 1))
+        def _():
+            join_pair(i, sign, buffers)
+            chain_copy(buffers, i, 0, 1, sign).start()
+            chain_copy(buffers, i, 0, 2, sign).start()
+
     def send_entering(i, sign, buffers):
         local, group, chain, leave, enter, state, usend, urecv, csend, crecv, dsend, drecv = buffers
         id_row = width + 1 if sign > 0 else width + 2
 
-        @pl.when(place(sign) < 2)
-        def _():
-            chain[0, i] = jnp.zeros((width + 8, width), F32)
-
-        @pl.when(place(sign) >= 2)
-        def _():
-            chain_copy(buffers, i, 0, 1, -sign).wait_recv()
-
-        @pl.when(latter(sign))
-        def _():
-            chain_copy(buffers, i, 1, 1, -sign).wait_recv()
-            mark = chain[1, i, width + 1 : width + 2, :]
-            factor = jnp.where(mark == chain[0, i, width + 1 : width + 2, :], chain[1, i, width : width + 1, :], 0.0)
-            entering = chain[0, i, 0:width] * factor + chain[1, i, 0:width]
-            chain[0, i, 0:width] = entering
-            chain[0, i, width:] = jnp.broadcast_to(mark, (8, width))
-            own = enter[i, width + 1 : width + 2, :]
-            factor = jnp.where(own == mark, enter[i, width : width + 1, :], 0.0)
-            enter[i, 0:width] = entering * factor + enter[i, 0:width]
-
-            @pl.when(place(sign) < groups - 1)
-            def _():
-                chain_copy(buffers, i, 0, 1, sign).start()
-                chain_copy(buffers, i, 0, 2, sign).start()
+        @pl.when(place(sign) == groups - 1)
+        def _():
+            join_pair(i, sign, buffers)
+
+        @pl.when(jnp.logical_not(latter(sign)))
+        def _():
+            receive_state(i, sign, buffers)
 
         carried = chain[0, i, 0:width]
         before = chain[0, i, width + 1 : width + 2, :]
@@ -300,19 +314,19 @@
             chain_copy(buffers, i, 0, 2, sign).wait_send()
 
     def scan(sign, buffers, part):
-        part(0)
-
         def steps(i, _):
             send_total(i, sign, buffers)
-
-            @pl.when(i < owned - 1)
+            part(i)
+            send_next(i, sign, buffers)
+
+            @pl.when(i > 0)
             def _():
-                part(i + 1)
-
-            send_entering(i, sign, buffers)
+                send_entering(i - 1, sign, buffers)
+
             return 0
 
         lax.fori_loop(0, owned, steps, 0)
+        send_entering(owned - 1, sign, buffers)
 
     def forward_part(i):
         for position in range(GROUP):

time: 69.6 us -> 69 us (level)
  no operation moved by 1% of the time
where the time goes in v4:
time: 69 us; the launch traced here: 68.8 us
  Pallas kernels  68.2 us (99%)
    pallas_call x1, Pallas kernels, per_device(): pl.pallas_call(functools.partial(kernel, nseq, nhead, float(heads * nhead...  64.6 us
    pallas_call x1, Pallas kernels, per_device(): pl.pallas_call(hand_over, out_shape=[rows] * 4, in_specs=[outside] * 4, o...  3.58 us

profile of v4, /device:TPU:0, one launch (start us, length us, event | category | flops | bytes accessed | tf_op | source)
XLA Modules:
  0.0 68.8 jit_solution(4445367266519217475)
XLA Ops:
  0.6 64.6 %shard_map.93 = (bf16[16,256,128]{2,1,0:T(8,128)(2,1)}, bf16[16,256,128]{2,1,0:T(8,128)(2,1)}, bf16[16,256,128]{2,1,0:T(8,128)(2,1)}, bf16[16,256,128]{2,1,0:T(8,128)(2,1)}) custom-call(bf16[16,256,128]{2,1,0:T(8,128)(2,1)} %q_in.1, bf16[16,256,128]{2,1,0:T(8,128)(2,1)} %k_in.1, bf16[16,256,128]{2,1,0:T(8,128)(2,1)} %v_in.1, f32[16,256]{1,0:T(8,128)} %gate_ref.1, ...), custom_call_target="tpu_custom_call" | custom-call | flops 2415919104 | bytes 8388608 | tf_op jit(solution)/shard_map/pallas_call | solution.py:532
  65.2 3.6 %shard_map.94 = (bf16[16,256,128]{2,1,0:T(8,128)(2,1)}, bf16[16,256,128]{2,1,0:T(8,128)(2,1)}, bf16[16,256,128]{2,1,0:T(8,128)(2,1)}, bf16[16,256,128]{2,1,0:T(8,128)(2,1)}) custom-call(bf16[16,256,128]{2,1,0:T(8,128)(2,1)} %get-tuple-element.8.refs_0_, bf16[16,256,128]{2,1,0:T(8,128)(2,1)} %get-tuple-element.9.refs_1_, ...), custom_call_target="tpu_custom_call" | custom-call | tf_op jit(solution)/shard_map/pallas_call | solution.py:581

commit v5 on v4

--- a/solution.py
+++ b/solution.py
@@ -27,10 +27,10 @@
     q_ref, k_ref, v_ref, go_ref, normed_ref, gq_ref, gk_ref, gv_ref,
     run_ref, runc_ref, grow_ref, fall_ref, pass_ref, allow_ref, epc_ref, decay_ref, score_ref,
     att_ref, gattn_ref, kin_ref, vin_ref, sums_ref, stat_ref, other_ref, norm_ref, corr_ref,
-    ids_ref, prev_ref, next_ref,
+    ids_ref, prev_ref, next_ref, marks_ref, group_marks_ref,
     local_ref, group_ref, chain_ref, leave_ref, enter_ref, state_ref,
     blocal_ref, bgroup_ref, bchain_ref, bleave_ref, benter_ref, bstate_ref,
-    in_sem, out_sem, gk_sem, gv_sem, id_send, id_recv, stat_send, stat_recv,
+    marks_send, marks_recv, in_sem, out_sem, gk_sem, gv_sem, id_send, id_recv, stat_send, stat_recv,
     up_send, up_recv, chain_send, chain_recv, down_send, down_recv,
     bup_send, bup_recv, bchain_send, bchain_recv, bdown_send, bdown_recv,
 ):
@@ -105,7 +105,10 @@
     half = lax.broadcasted_iota(jnp.int32, (8, width), 1) < width // 2
     ids_ref[...] = jnp.where(half, first_id, last_id)
     row = lax.broadcasted_iota(jnp.int32, (8, width), 0)
-    id_rows = jnp.where(row == 1, last_id, first_id)
+    for position in range(GROUP):
+        marks_ref[position] = jnp.where(row == owned, last_id, first_id)
+        marks_ref[position, 0:owned] = pass_ref[position * owned : (position + 1) * owned, :]
+    group_marks_ref[c] = marks_ref[c]
     loads[0].wait()
     loads[1].wait()
 
@@ -113,8 +116,7 @@
         h = position * owned + i
         weight = jnp.where(epc_ref[...] == last_id, fall_ref[h], 0.0)
         decayed = (k_ref[h].astype(F32) * weight).astype(BF16)
-        target[*at, 0:width] = product(decayed, v_ref[h], 0, 0)
-        target[*at, width:] = jnp.where(row == 0, pass_ref[pl.ds(h, 1), :], id_rows)
+        target[*at] = product(decayed, v_ref[h], 0, 0)
 
     def local_states(i):
         for d in (1, 2, 3):
@@ -174,7 +176,15 @@
         for d in (1, 2, 3):
             up_copy(local, group, usend, urecv, other(d), i).start()
 
+    def marks_copy(position, slot):
+        return remote(
+            marks_ref.at[position], group_marks_ref.at[slot], marks_send.at[position], marks_recv.at[slot],
+            member(position),
+        )
+
     send_local(0, forward_set)
+    for d in (1, 2, 3):
+        marks_copy(other(d), c).start()
 
     @pl.when(s < nseq - 1)
     def _():
@@ -217,18 +227,18 @@
 
     def send_total(i, sign, buffers):
         local, group, chain, leave, enter, state, usend, urecv, csend, crecv, dsend, drecv = buffers
-        id_row = width + 1 if sign > 0 else width + 2
+        id_row = owned if sign > 0 else owned + 1
         for d in range(1, GROUP):
             up_arrival(local, group, usend, urecv, other(d), i).wait_recv()
         total_state = None
         for j in range(GROUP)[::sign]:
-            factor = group[j, i, width : width + 1, :]
-            mark = group[j, i, id_row : id_row + 1, :]
+            factor = group_marks_ref[j, pl.ds(i, 1), :]
+            mark = group_marks_ref[j, id_row : id_row + 1, :]
             if total_state is None:
-                total_state = group[j, i, 0:width]
+                total_state = group[j, i]
                 factors = factor
             else:
-                total_state = total_state * jnp.where(mark == before, factor, 0.0) + group[j, i, 0:width]
+                total_state = total_state * jnp.where(mark == before, factor, 0.0) + group[j, i]
                 factors = factors * factor
             before = mark
         enter[i, 0:width] = total_state
@@ -271,7 +281,7 @@
 
     def send_entering(i, sign, buffers):
         local, group, chain, leave, enter, state, usend, urecv, csend, crecv, dsend, drecv = buffers
-        id_row = width + 1 if sign > 0 else width + 2
+        id_row = owned if sign > 0 else owned + 1
 
         @pl.when(place(sign) == groups - 1)
         def _():
@@ -286,9 +296,9 @@
         for n, j in enumerate(range(GROUP)[::sign]):
             leave[j, i] = carried
             if n < GROUP - 1:
-                mark = group[j, i, id_row : id_row + 1, :]
-                factor = jnp.where(mark == before, group[j, i, width : width + 1, :], 0.0)
-                carried = carried * factor + group[j, i, 0:width]
+                mark = group_marks_ref[j, id_row : id_row + 1, :]
+                factor = jnp.where(mark == before, group_marks_ref[j, pl.ds(i, 1), :], 0.0)
+                carried = carried * factor + group[j, i]
                 before = mark
         for d in range(1, GROUP):
             down_copy(leave, state, dsend, drecv, other(d), i).start()
@@ -339,6 +349,8 @@
             att_ref[h] = product(score, v_ref[h], 1, 0)
 
     loads[2].wait()
+    for d in (1, 2, 3):
+        marks_copy(other(d), other(d)).wait()
     scan(1, forward_set, forward_part)
 
     @pl.when(s == 0)
@@ -417,13 +429,10 @@
             weight = jnp.where(epc_ref[...] == first_id, grow_ref[h], 0.0)
             decayed = (q_ref[h].astype(F32) * weight).astype(BF16)
             value = product(decayed, grad, 0, 0)
-            below_rows = jnp.where(row == 0, pass_ref[pl.ds(h, 1), :], id_rows)
             if d == 0:
-                bgroup_ref[c, i, 0:width] = value
-                bgroup_ref[c, i, width:] = below_rows
+                bgroup_ref[c, i] = value
             else:
-                blocal_ref[h, 0:width] = value
-                blocal_ref[h, width:] = below_rows
+                blocal_ref[h] = value
                 up_copy(blocal_ref, bgroup_ref, bup_send, bup_recv, position, i).start()
         return 0
 
@@ -513,8 +522,8 @@
     rows = jax.ShapeDtypeStruct(query_rows.shape, BF16)
     block = (heads, tokens, width)
     state_set = [
-        pltpu.VMEM((heads, width + 8, width), F32),
-        pltpu.VMEM((GROUP, owned, width + 8, width), F32),
+        pltpu.VMEM((heads, width, width), F32),
+        pltpu.VMEM((GROUP, owned, width, width), F32),
         pltpu.VMEM((2, owned, width + 8, width), F32),
         pltpu.VMEM((GROUP, owned, width, width), F32),
         pltpu.VMEM((owned, width + 8, width), F32),
@@ -557,8 +566,12 @@
             pltpu.VMEM((8, width), F32),
             pltpu.VMEM((8, width), F32),
             pltpu.VMEM((8, width), F32),
+            pltpu.VMEM((GROUP, 8, width), F32),
+            pltpu.VMEM((GROUP, 8, width), F32),
             *state_set,
             *state_set,
+            pltpu.SemaphoreType.DMA((GROUP,)),
+            pltpu.SemaphoreType.DMA((GROUP,)),
             pltpu.SemaphoreType.DMA((4,)),
             pltpu.SemaphoreType.DMA((2,)),
             pltpu.SemaphoreType.DMA((heads,)),

time: 69 us -> 69 us (level)
  no operation moved by 1% of the time
where the time goes in v5:
time: 69 us; the launch traced here: 68.8 us
  Pallas kernels  68.1 us (99%)
    pallas_call x1, Pallas kernels, per_device(): pl.pallas_call(functools.partial(kernel, nseq, nhead, float(heads * nhead...  64.5 us
    pallas_call x1, Pallas kernels, per_device(): pl.pallas_call(hand_over, out_shape=[rows] * 4, in_specs=[outside] * 4, o...  3.58 us

profile of v5, /device:TPU:0, one launch (start us, length us, event | category | flops | bytes accessed | tf_op | source)
XLA Modules:
  0.0 68.8 jit_solution(6534174498156244503)
XLA Ops:
  0.6 64.5 %shard_map.93 = (bf16[16,256,128]{2,1,0:T(8,128)(2,1)}, bf16[16,256,128]{2,1,0:T(8,128)(2,1)}, bf16[16,256,128]{2,1,0:T(8,128)(2,1)}, bf16[16,256,128]{2,1,0:T(8,128)(2,1)}) custom-call(bf16[16,256,128]{2,1,0:T(8,128)(2,1)} %q_in.1, bf16[16,256,128]{2,1,0:T(8,128)(2,1)} %k_in.1, bf16[16,256,128]{2,1,0:T(8,128)(2,1)} %v_in.1, f32[16,256]{1,0:T(8,128)} %gate_ref.1, ...), custom_call_target="tpu_custom_call" | custom-call | flops 2415919104 | bytes 8388608 | tf_op jit(solution)/shard_map/pallas_call | solution.py:541
  65.2 3.6 %shard_map.94 = (bf16[16,256,128]{2,1,0:T(8,128)(2,1)}, bf16[16,256,128]{2,1,0:T(8,128)(2,1)}, bf16[16,256,128]{2,1,0:T(8,128)(2,1)}, bf16[16,256,128]{2,1,0:T(8,128)(2,1)}) custom-call(bf16[16,256,128]{2,1,0:T(8,128)(2,1)} %get-tuple-element.8.refs_0_, bf16[16,256,128]{2,1,0:T(8,128)(2,1)} %get-tuple-element.9.refs_1_, ...), custom_call_target="tpu_custom_call" | custom-call | tf_op jit(solution)/shard_map/pallas_call | solution.py:594
